TPU v7x, 32 devices: a whole 2x2x4 slice. The times are simulated.
32 devices in a mesh: dp: 8 (over z, y), seq: 4 (over x, core).
Axes of the slice: x: 2, y: 2, z: 4, core: 2. Of those that a mesh axis runs over, the one named last changes fastest.
Arguments:
- frames: bfloat16 [4096, 1536], P('dp', 'seq')
- owner_slot: int32 [4096], P('dp'), may hold values from -1 to 4095, as said below
- segment: int32 [8, 512], P('dp'), may hold values from 0 to 2, never falling along the last dimension, each value on 1 to 256 neighbouring positions
- norm_gain: float32 [1536], replicated, may hold values from 0.25 to 1.75
- expand: bfloat16 [1536, 2, 1536], P('dp', None, 'seq'), may hold values from -0.15625 to 0.15625
- kernel: float32 [9, 1536], P(None, 'seq'), may hold values from -2.5 to 2.5
- project: bfloat16 [1536, 1536], P('seq', 'dp'), may hold values from -0.15625 to 0.15625
- cotangent: bfloat16 [4096, 1536], P('dp', 'seq'), may hold values from -6 to 6
Outputs:
- output: bfloat16 [4096, 1536], P('dp', 'seq')
- grad_frames: bfloat16 [4096, 1536], P('dp', 'seq')
- grad_gain: float32 [1536], P('seq')
- grad_kernel: float32 [9, 1536], P(None, 'seq')
- grad_expand: float32 [1536, 2, 1536], P('dp', None, 'seq')
- grad_project: float32 [1536, 1536], P('seq', 'dp')
Inputs may be any that keep to these rules, and one draw needn't show every extreme that they name: `owner_slot`: for each arrival row, the balanced row that takes it, or -1 for an empty arrival row; no balanced row is named twice. The live rows of each pack come first, contiguous, ordered by sending index of dp and then by arrival row; empty rows fill the pack's tail. Of the 512 arrival rows of one index of dp, at most 64 name rows of any one pack; some pack takes exactly 64 rows from every index of dp. `segment`: within each pack the utterance numbers never fall; a pack holds 3 utterances of 1 to 256 frames, one of exactly 256.
All inputs are finite; a program needn't handle non-finite values.
Results may differ from a plain program's by a relative error of at most 0.01.
Values may be sent and summed in bfloat16 or wider, within the bound.
A program may use at most 128 MiB of HBM per device.

v0:
```python
import math

import jax
import jax.numpy as jnp
from jax import lax
from jax.sharding import PartitionSpec as P

D = 1536
KSIZE = 9


EPS = 1e-05


def conv_masks(labels):
    half_width = (KSIZE - 1) // 2
    length = labels.shape[0]
    padded = jnp.pad(labels, (half_width, half_width), constant_values=-1)
    return [
        (padded[tap_index : tap_index + length] == labels).astype(jnp.float32)[:, None]
        for tap_index in range(KSIZE)
    ]


def depthwise(signal, kernel, tap_masks):
    half_width = (KSIZE - 1) // 2
    length = signal.shape[0]
    padded = jnp.pad(signal, ((half_width, half_width), (0, 0)))
    total = jnp.zeros(signal.shape, jnp.float32)
    for tap_index in range(KSIZE):
        total = (
            total
            + kernel[tap_index] * padded[tap_index : tap_index + length] * tap_masks[tap_index]
        )
    return total


def depthwise_back(signal, upstream, kernel, tap_masks):
    half_width = (KSIZE - 1) // 2
    length = signal.shape[0]
    padded = jnp.pad(signal, ((half_width, half_width), (0, 0)))
    spread = jnp.zeros((length + 2 * half_width, signal.shape[1]), jnp.float32)
    tap_sums = []
    for tap_index in range(KSIZE):
        masked = upstream * tap_masks[tap_index]
        tap_sums.append(jnp.sum(masked * padded[tap_index : tap_index + length], axis=0))
        spread = spread + jnp.pad(
            kernel[tap_index] * masked, ((tap_index, 2 * half_width - tap_index), (0, 0))
        )
    return (jnp.stack(tap_sums), spread[half_width : half_width + length])


def place_rows(incoming, landing, row_count):
    flat = incoming.reshape(-1, incoming.shape[-1])
    total_slots = flat.shape[0]
    inverse = (
        jnp.full((row_count + 1,), total_slots, jnp.int32)
        .at[landing.reshape(-1)]
        .set(jnp.arange(total_slots, dtype=jnp.int32))[:row_count]
    )
    padded = jnp.concatenate([flat, jnp.zeros((1, flat.shape[1]), flat.dtype)])
    return (padded[inverse], inverse < total_slots)


def shards(frames, owner_slot, segment, norm_gain, expand, kernel, project, cotangent):
    row_count, quarter = frames.shape
    groups = lax.axis_size("dp")
    lane_index = lax.axis_index("seq")
    capacity = row_count // groups
    bucket_slots = groups * capacity
    dest_group = jnp.where(owner_slot >= 0, owner_slot // row_count, groups)
    onehot = (dest_group[:, None] == jnp.arange(groups, dtype=jnp.int32)[None, :]).astype(jnp.int32)
    earlier = jnp.cumsum(onehot, axis=0) - onehot
    within = jnp.sum(earlier * onehot, axis=1)
    send_pos = jnp.where(owner_slot >= 0, dest_group * capacity + within, bucket_slots)
    source_row = (
        jnp.full((bucket_slots + 1,), row_count, jnp.int32)
        .at[send_pos]
        .set(jnp.arange(row_count, dtype=jnp.int32))[:bucket_slots]
    )
    slot_padded = jnp.concatenate([owner_slot, jnp.full((1,), -1, jnp.int32)])
    named_slot = slot_padded[source_row]
    landing_out = jnp.where(named_slot >= 0, named_slot % row_count, row_count).reshape(
        groups, capacity
    )
    padded_in = jnp.concatenate([frames, jnp.zeros((1, quarter), jnp.bfloat16)])
    outgoing = padded_in[source_row].reshape(groups, capacity, quarter)
    incoming, landing = (
        lax.all_to_all(outgoing, "dp", split_axis=0, concat_axis=0, tiled=True),
        lax.all_to_all(landing_out, "dp", split_axis=0, concat_axis=0, tiled=True),
    )
    local_rows, occupied = place_rows(incoming, landing, row_count)
    whole_rows = lax.all_gather(local_rows, "seq", axis=1, tiled=True)
    live_col = occupied.astype(jnp.float32)[:, None]
    floats = whole_rows.astype(jnp.float32)
    row_mean = jnp.mean(floats, axis=1, keepdims=True)
    centred = floats - row_mean
    inv_scale = lax.rsqrt(jnp.mean(centred * centred, axis=1, keepdims=True) + EPS)
    normed = centred * inv_scale
    scaled = (normed * norm_gain).astype(jnp.bfloat16)
    expand_full = lax.all_gather(expand, "dp", axis=0, tiled=True).reshape(D, 2 * quarter)
    project_full = lax.all_gather(project, "dp", axis=1, tiled=True)
    joined = jnp.dot(scaled, expand_full, preferred_element_type=jnp.float32)
    value_half = joined[:, :quarter]
    gate_sig = jax.nn.sigmoid(joined[:, quarter:])
    glu_out = value_half * gate_sig
    tap_masks = conv_masks(segment[0])
    conv_out = depthwise(glu_out, kernel, tap_masks)
    conv_sig = jax.nn.sigmoid(conv_out)
    hidden = (conv_out * conv_sig * live_col).astype(jnp.bfloat16)
    partial_out = jnp.dot(hidden, project_full, preferred_element_type=jnp.float32)
    mixed_share = lax.psum_scatter(
        partial_out.astype(jnp.bfloat16), "seq", scatter_dimension=1, tiled=True
    ).astype(jnp.float32)
    output = (local_rows.astype(jnp.float32) + mixed_share).astype(jnp.bfloat16)
    inv_root = 1.0 / math.sqrt(row_count * groups)
    cot_full = lax.all_gather(cotangent, "seq", axis=1, tiled=True)
    project_term = lax.dot_general(
        hidden, cot_full, (((0,), (0,)), ((), ())), preferred_element_type=jnp.float32
    )
    grad_project = lax.psum_scatter(project_term, "dp", scatter_dimension=1, tiled=True) * inv_root
    hidden_grad = (
        lax.dot_general(
            cot_full, project_full, (((1,), (1,)), ((), ())), preferred_element_type=jnp.float32
        )
        * live_col
    )
    conv_grad = hidden_grad * (conv_sig + conv_out * conv_sig * (1.0 - conv_sig))
    kernel_term, glu_grad = depthwise_back(glu_out, conv_grad, kernel, tap_masks)
    proj_grad = jnp.concatenate(
        [glu_grad * gate_sig, glu_grad * value_half * gate_sig * (1.0 - gate_sig)], axis=1
    ).astype(jnp.bfloat16)
    term_block = lax.dot_general(
        scaled, proj_grad, (((0,), (0,)), ((), ())), preferred_element_type=jnp.float32
    )
    grad_expand = (
        lax.psum_scatter(
            term_block.reshape(expand.shape[0] * lax.axis_size("dp"), 2, quarter),
            "dp",
            scatter_dimension=0,
            tiled=True,
        )
        * inv_root
    )
    scaled_part = lax.dot_general(
        proj_grad, expand_full, (((1,), (1,)), ((), ())), preferred_element_type=jnp.float32
    )
    normed_local = lax.dynamic_slice_in_dim(normed, lane_index * quarter, quarter, 1)
    scaled_grad = lax.psum(scaled_part.astype(jnp.bfloat16), "seq").astype(jnp.float32)
    normed_grad = scaled_grad * norm_gain
    first_mean = jnp.mean(normed_grad, axis=1, keepdims=True)
    second_mean = jnp.mean(normed_grad * normed, axis=1, keepdims=True)
    full_grad = inv_scale * (normed_grad - first_mean - normed * second_mean)
    packed_grad = lax.dynamic_slice_in_dim(full_grad, lane_index * quarter, quarter, 1)
    scaled_share = lax.dynamic_slice_in_dim(scaled_grad, lane_index * quarter, quarter, 1)
    gain_term = jnp.sum(scaled_share * normed_local, axis=0)
    gain_sum, kernel_sum = lax.psum((gain_term, kernel_term), "dp")
    back_rows = (packed_grad + cotangent.astype(jnp.float32)).astype(jnp.bfloat16)
    back_padded = jnp.concatenate([back_rows, jnp.zeros((1, quarter), jnp.bfloat16)])
    returning = back_padded[landing.reshape(-1)].reshape(groups, capacity, quarter)
    returned = lax.all_to_all(returning, "dp", split_axis=0, concat_axis=0, tiled=True)
    returned_flat = jnp.concatenate(
        [returned.reshape(bucket_slots, quarter), jnp.zeros((1, quarter), jnp.bfloat16)]
    )
    grad_frames = returned_flat[send_pos]
    return (
        output,
        grad_frames,
        gain_sum * inv_root,
        kernel_sum * inv_root,
        grad_expand,
        grad_project,
    )


def solution(mesh):
    placed = (
        P("dp", "seq"),
        P("dp"),
        P("dp", None),
        P(),
        P("dp", None, "seq"),
        P(None, "seq"),
        P("seq", "dp"),
        P("dp", "seq"),
    )
    return jax.shard_map(
        shards,
        mesh=mesh,
        in_specs=placed,
        out_specs=(
            P("dp", "seq"),
            P("dp", "seq"),
            P("seq"),
            P(None, "seq"),
            P("dp", None, "seq"),
            P("seq", "dp"),
        ),
        check_vma=False,
    )
```

profile of v0, /device:TPU:9, one launch (start us, length us, event | category | flops | bytes accessed | tf_op | source)
XLA Modules:
  0.0 521.1 jit_solution(7484022460435981504)
XLA Ops:
  10.8 2.4 scatter_custom_fusion
  17.0 5.7 %all-to-all-start.1 = ((s32[8,1,64]{2,1,0:T(1,128)}), s32[8,1,64]{2,1,0:T(1,128)S(1)}, u32[]{:S(2)}, u32[]{:S(2)}) async-start(s32[8,1,64]{2,1,0:T(1,128)} %compare_select_fusion.2), calls=%async_computation.1 | async-start | bytes 8192 | tf_op jit(solution)/shard_map/all_to_all | solution.py:90
  22.8 2.6 gather_fusion
  26.7 4.6 all-to-all-start
  32.6 2.4 scatter_custom_fusion.1
  35.1 4.1 all-to-all-done
  39.3 2.6 gather_fusion.2
  44.3 20.6 %all-gather.12.cloned.1.call-done = bf16[512,1536]{1,0:T(8,128)(2,1)} async-done(((bf16[512,384]{1,0:T(8,128)(2,1)}), bf16[512,1536]{1,0:T(8,128)(2,1)}) %all-gather.12.cloned.1.call-update) | async-done | bytes 1572880 | tf_op jit(solution)/shard_map/all_gather | solution.py:93
  67.4 50.4 %all-gather.6.cloned.1.call-done = bf16[1536,2,384]{2,1,0:T(2,128)(2,1)} async-done(((bf16[192,2,384]{2,1,0:T(2,128)(2,1)}), bf16[1536,2,384]{2,1,0:T(2,128)(2,1)}) %all-gather.6.cloned.1.call-update) | async-done | bytes 2359312 | tf_op jit(solution)/shard_map/all_gather | solution.py:101
  124.6 34.6 %all-gather.8.cloned.1.call-done = bf16[384,1536]{0,1:T(8,128)(2,1)} async-done(((bf16[384,192]{0,1:T(8,128)(2,1)}), bf16[384,1536]{0,1:T(8,128)(2,1)}) %all-gather.8.cloned.1.call-update) | async-done | bytes 1179664 | tf_op jit(solution)/shard_map/all_gather | solution.py:102
  159.3 21.7 %all-gather.10.cloned.1.call-done = bf16[512,1536]{1,0:T(8,128)(2,1)} async-done(((bf16[512,384]{1,0:T(8,128)(2,1)}), bf16[512,1536]{1,0:T(8,128)(2,1)}) %all-gather.10.cloned.1.call-update) | async-done | bytes 1572880 | tf_op jit(solution)/shard_map/all_gather | solution.py:117
  180.9 8.1 %multiply_reduce_fusion.1 = (f32[384]{0:T(512)}, f32[384]{0:T(512)}, f32[384]{0:T(512)}, f32[384]{0:T(512)}, f32[384]{0:T(512)}, /*index=5*/f32[384]{0:T(512)}, ...) fusion(f32[512,384]{1,0:T(8,128)} %copy-done.3, ...), kind=kOutput, calls=%fused_computation.36 | convolution fusion | flops 611054208 | bytes 5932032 | tf_op jit(solution)/shard_map/dot_general | solution.py:123
  192.3 2.6 convolution_convert_fusion
  195.0 2.6 convolution_convert_fusion.1
  199.3 4.3 fusion.44
  204.6 3.8 fusion.12
  208.4 8.2 %copy.16 = f32[1536,2,384]{2,1,0:T(2,128)} copy(f32[1536,2,384]{0,2,1:T(8,128)} %bitcast.29) | data formatting | bytes 9437184 | tf_op jit(solution)/shard_map/reshape | solution.py:138
  217.2 20.2 %all-reduce.20.cloned.1.call-done = bf16[512,1536]{1,0:T(8,128)(2,1)} async-done(((bf16[512,1536]{1,0:T(8,128)(2,1)}), bf16[512,1536]{1,0:T(8,128)(2,1)}) %all-reduce.20.cloned.1.call-update) | async-done | bytes 1572880 | tf_op jit(solution)/shard_map/psum | solution.py:149
  240.9 2.6 gather_fusion.3
  243.5 5.5 %all-to-all-start.2 = ((bf16[8,64,384]{2,1,0:T(8,128)(2,1)}), bf16[8,64,384]{2,1,0:T(8,128)(2,1)S(1)}, u32[]{:S(2)}, u32[]{:S(2)}) async-start(bf16[8,64,384]{2,1,0:T(8,128)(2,1)} %bitcast.7), calls=%async_computation.2 | async-start | bytes 786432 | tf_op jit(solution)/shard_map/all_to_all | solution.py:161
  250.5 27.4 %all-reduce.16 = (f32[384]{0:T(512)S(1)}, f32[9,384]{1,0:T(8,128)S(1)}) all-reduce(f32[384]{0:T(512)S(1)} %get-tuple-element.30, f32[9,384]{1,0:T(8,128)S(1)} %stack.39), channel_id=1, replica_groups=mesh['dp'=8,'seq'=4] {'dp'}, use_global_device_ids=true, to_apply=%region_12.13 | all-reduce | flops 3840 | bytes 30720 | tf_op jit(solution)/shard_map/psum | solution.py:157
  279.2 2.6 gather_fusion.4
  283.8 55.6 %reduce-scatter.5.cloned.1.call-done = f32[384,192]{0,1:T(8,128)} async-done(((f32[384,1536]{0,1:T(8,128)}), f32[384,192]{0,1:T(8,128)}) %reduce-scatter.5.cloned.1.call-update) | async-done | bytes 294928 | tf_op jit(solution)/shard_map/reduce_scatter | solution.py:121
  341.1 171.0 %all-reduce.22.cloned.1.call-done = f32[1536,2,384]{2,1,0:T(2,128)} async-done(((f32[1536,2,384]{2,1,0:T(2,128)}), f32[1536,2,384]{2,1,0:T(2,128)}) %all-reduce.22.cloned.1.call-update) | async-done | bytes 4718608
  (141 shorter events, 39.6 us)
Async XLA Ops:
  7.2 15.5 %copy-start.7 = (bf16[512,384]{1,0:T(8,128)(2,1)S(1)}, bf16[512,384]{1,0:T(8,128)(2,1)}, u32[]{:S(2)}) copy-start(bf16[512,384]{1,0:T(8,128)(2,1)} %param.8) | copy-start | bytes 1179652
  17.0 9.8 %all-to-all-start.1 = ((s32[8,1,64]{2,1,0:T(1,128)}), s32[8,1,64]{2,1,0:T(1,128)S(1)}, u32[]{:S(2)}, u32[]{:S(2)}) async-start(s32[8,1,64]{2,1,0:T(1,128)} %compare_select_fusion.2), calls=%async_computation.1 | async-start | bytes 8192 | tf_op jit(solution)/shard_map/all_to_all | solution.py:90
  26.7 12.5 %all-to-all-start = ((bf16[8,64,384]{2,1,0:T(8,128)(2,1)}), bf16[8,64,384]{2,1,0:T(8,128)(2,1)S(1)}, u32[]{:S(2)}, u32[]{:S(2)}) async-start(bf16[8,64,384]{2,1,0:T(8,128)(2,1)} %bitcast.3), calls=%async_computation | async-start | bytes 786432 | tf_op jit(solution)/shard_map/all_to_all | solution.py:89
  31.3 33.7 %all-gather.12.cloned.1.call-start = ((), (), s32[]{:S(2)}) async-start(), calls=%async_computation.10 | async-start | bytes 1966080 | tf_op jit(solution)/shard_map/all_gather | solution.py:93
  41.9 75.9 %all-gather.6.cloned.1.call-start = ((), (), s32[]{:S(2)}) async-start(), calls=%async_computation.5 | async-start | bytes 2654208 | tf_op jit(solution)/shard_map/all_gather | solution.py:101
  42.6 116.6 %all-gather.8.cloned.1.call-start = ((), (), s32[]{:S(2)}) async-start(), calls=%async_computation.6 | async-start | bytes 1327104 | tf_op jit(solution)/shard_map/all_gather | solution.py:102
  43.4 137.6 %all-gather.10.cloned.1.call-start = ((), (), s32[]{:S(2)}) async-start(), calls=%async_computation.7 | async-start | bytes 1966080 | tf_op jit(solution)/shard_map/all_gather | solution.py:117
  43.9 193.5 %all-reduce.20.cloned.1.call-start = ((), (), s32[]{:S(2)}) async-start(), calls=%async_computation.8 | async-start | bytes 3145728 | tf_op jit(solution)/shard_map/psum | solution.py:149
  44.3 136.6 %copy-start.26 = (f32[512]{0:T(512)}, f32[512]{0:T(512)S(1)}, u32[]{:S(2)}) copy-start(f32[512]{0:T(512)S(1)} %compare_convert_fusion) | copy-start | bytes 6148
  194.9 86.8 %reduce-scatter.7.cloned.1.call-start = ((), (), s32[]{:S(2)}) async-start(), calls=%async_computation.11 | async-start | bytes 1966080
  199.2 140.2 %reduce-scatter.5.cloned.1.call-start = ((), (), s32[]{:S(2)}) async-start(), calls=%async_computation.9 | async-start | bytes 2654208 | tf_op jit(solution)/shard_map/reduce_scatter | solution.py:121
  203.6 308.4 %all-reduce.22.cloned.1.call-start = ((), (), s32[]{:S(2)}) async-start(), calls=%async_computation.12 | async-start | bytes 9437184
  240.8 8.2 %copy-start.27 = (u32[32]{0:T(128)S(1)}, u32[32]{0:T(128)}, u32[]{:S(2)}) copy-start(u32[32]{0:T(128)} %constant.108) | copy-start | bytes 388
  240.8 9.4 %copy-start.12 = (s32[512]{0:T(512)S(1)}, s32[512]{0:T(512)}, u32[]{:S(2)}) copy-start(s32[512]{0:T(512)} %copy-done.11) | copy-start | bytes 6148
  240.9 9.4 %copy-start.25 = (f32[384]{0:T(512)S(1)}, f32[384]{0:T(512)}, u32[]{:S(2)}) copy-start(f32[384]{0:T(512)} %get-tuple-element.9) | copy-start | bytes 4612
  240.9 9.4 %copy-start.24 = (f32[384]{0:T(512)S(1)}, f32[384]{0:T(512)}, u32[]{:S(2)}) copy-start(f32[384]{0:T(512)} %get-tuple-element.10) | copy-start | bytes 4612
  240.9 9.4 %copy-start.23 = (f32[384]{0:T(512)S(1)}, f32[384]{0:T(512)}, u32[]{:S(2)}) copy-start(f32[384]{0:T(512)} %get-tuple-element.11) | copy-start | bytes 4612
  240.9 9.5 %copy-start.22 = (f32[384]{0:T(512)S(1)}, f32[384]{0:T(512)}, u32[]{:S(2)}) copy-start(f32[384]{0:T(512)} %get-tuple-element.12) | copy-start | bytes 4612
  240.9 9.5 %copy-start.21 = (f32[384]{0:T(512)S(1)}, f32[384]{0:T(512)}, u32[]{:S(2)}) copy-start(f32[384]{0:T(512)} %get-tuple-element.16) | copy-start | bytes 4612
  240.9 9.5 %copy-start.20 = (f32[384]{0:T(512)S(1)}, f32[384]{0:T(512)}, u32[]{:S(2)}) copy-start(f32[384]{0:T(512)} %get-tuple-element.13) | copy-start | bytes 4612
  240.9 9.5 %copy-start.19 = (f32[384]{0:T(512)S(1)}, f32[384]{0:T(512)}, u32[]{:S(2)}) copy-start(f32[384]{0:T(512)} %get-tuple-element.14) | copy-start | bytes 4612
  240.9 9.5 %copy-start.18 = (f32[384]{0:T(512)S(1)}, f32[384]{0:T(512)}, u32[]{:S(2)}) copy-start(f32[384]{0:T(512)} %get-tuple-element.15) | copy-start | bytes 4612
  240.9 9.5 %copy-start.17 = (f32[384]{0:T(512)S(1)}, f32[384]{0:T(512)}, u32[]{:S(2)}) copy-start(f32[384]{0:T(512)} %get-tuple-element.8) | copy-start | bytes 4612
  243.5 35.6 %all-to-all-start.2 = ((bf16[8,64,384]{2,1,0:T(8,128)(2,1)}), bf16[8,64,384]{2,1,0:T(8,128)(2,1)S(1)}, u32[]{:S(2)}, u32[]{:S(2)}) async-start(bf16[8,64,384]{2,1,0:T(8,128)(2,1)} %bitcast.7), calls=%async_computation.2 | async-start | bytes 786432 | tf_op jit(solution)/shard_map/all_to_all | solution.py:161
  (15 other events, 40.2 us)
Sparse Core Ops, SparseCore 0:
  42.0 22.9 all-gather.11
  67.1 50.6 all-gather.5
  120.0 39.2 all-gather.7
  160.7 20.2 all-gather.9
  195.0 42.3 all-reduce.19
  239.8 28.3 reduce-scatter.6
  272.1 67.3 reduce-scatter.4
  343.5 168.5 all-reduce.21
where the time goes:
time: 526 us; the launch traced here: 521 us
  waiting for transfers between devices  382 us (73%)
  local copies, waits for them, and re-layouts  36.4 us (7%)
  blocking collectives  27.4 us (5%)
  matrix products  22.8 us (4%)
  other arithmetic  21 us (4%)
  starting transfers between devices  16.5 us (3%)
  between operations  15.4 us (3%)
    unnamed x10, waiting for transfers between devices  173 us
    reduce_scatter x1, waiting for transfers between devices, shards(): lax.psum_scatter(project_term, 'dp', scatter_dimension=1, tiled=True)  55.6 us
    all_gather x1, waiting for transfers between devices, shards(): lax.all_gather(expand, 'dp', axis=0, tiled=True).reshape(D, 2 * quarter)  50.4 us
    all_gather x1, waiting for transfers between devices, shards(): project_full = lax.all_gather(project, 'dp', axis=1, tiled=True)  34.6 us
    psum x1, blocking collectives, shards(): gain_sum, kernel_sum = lax.psum((gain_term, kernel_term), 'dp')  27.4 us
    all_gather x1, waiting for transfers between devices, shards(): cot_full = lax.all_gather(cotangent, 'seq', axis=1, tiled=True)  21.7 us
    all_gather x1, waiting for transfers between devices, shards(): whole_rows = lax.all_gather(local_rows, 'seq', axis=1, tiled=True)  20.6 us
    psum x1, waiting for transfers between devices, shards(): lax.psum(scaled_part.astype(jnp.bfloat16), 'seq').astype(jnp.float32)  20.2 us
  transfers between devices with their start and end apart: 11, of which 9 were waited for; matrix products, arithmetic and copies ran while one was open for 9% of the time, Pallas kernels for 0%

commit v1 on v0

v1 whole, which is shorter than its diff:
```python
import functools
import math

import jax
import jax.numpy as jnp
from jax import lax
from jax.experimental import pallas as pl
from jax.experimental.pallas import tpu as pltpu
from jax.sharding import PartitionSpec as P

D = 1536
KSIZE = 9
HALF = KSIZE // 2
EPS = 1e-05
BF16 = jnp.bfloat16
F32 = jnp.float32
NT = (((1,), (1,)), ((), ()))
TN = (((0,), (0,)), ((), ()))


def dot(a, b, dims=(((1,), (0,)), ((), ())), precision=None):
    return lax.dot_general(a, b, dims, preferred_element_type=F32, precision=precision)


def span(index, size):
    return pl.ds(pl.multiple_of(index * size, size), size)


def enter(groups, lanes):
    me, lane = lax.axis_index("dp"), lax.axis_index("seq")
    barrier = pltpu.get_barrier_semaphore()

    def greet_group(k, carry):
        pl.semaphore_signal(barrier, inc=1, device_id=(lax.rem(me + k, groups), lane),
                            device_id_type=pl.DeviceIdType.MESH)
        return carry

    def greet_lane(k, carry):
        pl.semaphore_signal(barrier, inc=1, device_id=(me, lax.rem(lane + k, lanes)),
                            device_id_type=pl.DeviceIdType.MESH)
        return carry

    lax.fori_loop(1, groups, greet_group, 0)
    lax.fori_loop(1, lanes, greet_lane, 0)
    pl.semaphore_wait(barrier, groups + lanes - 2)


def remote(src, dst, sems, k, device):
    return pltpu.make_async_remote_copy(
        src_ref=src, dst_ref=dst, send_sem=sems.at[0, k], recv_sem=sems.at[1, k],
        device_id=device, device_id_type=pl.DeviceIdType.MESH)


def each(first, last, body):
    def step(k, carry):
        body(k)
        return carry

    lax.fori_loop(first, last, step, 0)


def arrive_kernel(groups, lanes, cap,
                  owner_ref, frames_ref, weight_ref, cot_ref,
                  local_ref, whole_ref, cot_full_ref, weight_full_ref, pick_ref, place_ref, total_ref,
                  outgoing, incoming, owners, row_sem, owner_sem, outer_sem, pair_sem, cot_sem, whole_sem, own_sem):
    rows, quarter = frames_ref.shape
    me, lane = lax.axis_index("dp"), lax.axis_index("seq")
    outers = groups // 2
    outer, inner = me // 2, lax.rem(me, 2)
    mate = outer * 2 + 1 - inner
    enter(groups, lanes)

    def owner_copy(k):
        return remote(owner_ref, owners.at[me], owner_sem, k, (lax.rem(me + k, groups), lane))

    def row_copy(k):
        to = lax.rem(me + k, groups)
        return remote(outgoing.at[to], incoming.at[me], row_sem, k, (to, lane))

    def outer_copy(k):
        to = lax.rem(outer + k, outers) * 2 + inner
        return remote(weight_ref, weight_full_ref.at[me], outer_sem, k, (to, lane))

    def pair_copy(k):
        held = lax.rem(outer - k + outers, outers) * 2 + inner
        return remote(weight_full_ref.at[held], weight_full_ref.at[held], pair_sem, k, (mate, lane))

    def first_pair_copy():
        return remote(weight_ref, weight_full_ref.at[me], pair_sem, 0, (mate, lane))

    def cot_copy(k):
        return remote(cot_ref, cot_full_ref.at[:, span(lane, quarter)], cot_sem, k,
                      (me, lax.rem(lane + k, lanes)))

    def whole_copy(k):
        return remote(local_ref, whole_ref.at[:, span(lane, quarter)], whole_sem, k,
                      (me, lax.rem(lane + k, lanes)))

    each(1, groups, lambda k: owner_copy(k).start())
    own_weight = pltpu.make_async_copy(weight_ref, weight_full_ref.at[me], own_sem.at[0])
    own_weight.start()
    own_cot = pltpu.make_async_copy(cot_ref, cot_full_ref.at[:, span(lane, quarter)], own_sem.at[1])
    own_cot.start()

    slot = owner_ref[0:1, :]
    group_id = lax.broadcasted_iota(jnp.int32, (groups, rows), 0)
    named = jnp.where((slot >= group_id * rows) & (slot < group_id * rows + rows), 1.0, 0.0)
    before = jnp.where(lax.broadcasted_iota(jnp.int32, (rows, rows), 0)
                       < lax.broadcasted_iota(jnp.int32, (rows, rows), 1), 1.0, 0.0).astype(BF16)
    rank = dot(named.astype(BF16), before)
    base = group_id.astype(F32) * cap
    position = jnp.sum((rank + base + 1.0) * named, axis=0, keepdims=True) - 1.0
    slots = groups * cap
    pick = jnp.where(lax.broadcasted_iota(jnp.int32, (slots, rows), 0) == position.astype(jnp.int32), 1.0, 0.0).astype(BF16)
    pick_ref[...] = pick
    outgoing[...] = dot(pick, frames_ref[...]).astype(BF16).reshape(groups, cap, quarter)
    each(1, groups, lambda k: row_copy(k).start())
    first_pair_copy().start()
    each(1, outers, lambda k: outer_copy(k).start())
    each(1, lanes, lambda k: cot_copy(k).start())

    owners[me] = owner_ref[...]
    incoming[me] = outgoing[me]
    each(1, groups, lambda k: owner_copy(k).wait())
    mine = lax.broadcasted_iota(jnp.int32, (1, rows), 1) * 0 + me * rows
    total = jnp.zeros((1, 1), F32)
    row_id = lax.broadcasted_iota(jnp.int32, (cap, rows), 1).astype(F32)
    step_id = lax.broadcasted_iota(jnp.int32, (cap, rows), 0).astype(F32)
    for source in range(groups):
        theirs = owners[source][0:1, :]
        count = jnp.sum(jnp.where((theirs >= mine) & (theirs < mine + rows), 1.0, 0.0), axis=1, keepdims=True)
        hit = (row_id - step_id == total) & (step_id < count)
        place_ref[pl.ds(source * cap, cap), :] = jnp.where(hit, 1.0, 0.0).astype(BF16)
        total = total + count
    total_ref[...] = jnp.broadcast_to(total, total_ref.shape)
    each(1, groups, lambda k: row_copy(k).wait())
    local_ref[...] = dot(place_ref[...], incoming[...].reshape(slots, quarter), TN).astype(BF16)
    own_whole = pltpu.make_async_copy(local_ref, whole_ref.at[:, span(lane, quarter)], own_sem.at[2])
    own_whole.start()
    each(1, lanes, lambda k: whole_copy(k).start())

    def forward(k):
        outer_copy(k).wait_recv()
        pair_copy(k).start()

    each(1, outers, forward)
    each(1, outers, lambda k: outer_copy(k).wait_send())
    first_pair_copy().wait()
    each(1, outers, lambda k: pair_copy(k).wait())
    each(1, lanes, lambda k: cot_copy(k).wait())
    each(1, lanes, lambda k: whole_copy(k).wait())
    own_weight.wait()
    own_cot.wait()
    own_whole.wait()


def leave_kernel(groups, lanes, cap, scale,
                 terms_ref, scaled_ref, mixed_ref, tap_ref, cot_ref, normed_ref, inv_ref, gain_ref, local_ref, pick_ref, place_ref,
                 out_ref, frames_ref, small_ref, weight_ref,
                 pair_in, pair_sum, outer_in, scaled_in, mixed_in, small_in, small_out, sums_in, sums_out, returning, returned,
                 pair_sem, outer_sem, scaled_sem, mixed_sem, small_sem, sums_sem, row_sem):
    rows, quarter = local_ref.shape
    me, lane = lax.axis_index("dp"), lax.axis_index("seq")
    outers = groups // 2
    outer, inner = me // 2, lax.rem(me, 2)
    mate = outer * 2 + 1 - inner
    slots = groups * cap
    enter(groups, lanes)

    def pair_copy(k):
        at = lax.rem(outer + k, outers)
        return remote(terms_ref.at[at * 2 + 1 - inner], pair_in.at[at], pair_sem, k, (mate, lane))

    def outer_copy(k):
        at = lax.rem(outer + k, outers)
        return remote(pair_sum.at[at], outer_in.at[outer], outer_sem, k, (at * 2 + inner, lane))

    def lane_copy(src, dst, sems, k):
        to = lax.rem(lane + k, lanes)
        return remote(src.at[:, span(to, quarter)], dst.at[lane], sems, k, (me, to))

    def sums_copy(k):
        return remote(sums_out, sums_in.at[lane], sums_sem, k, (me, lax.rem(lane + k, lanes)))

    def small_copy(k):
        return remote(small_out, small_in.at[me], small_sem, k, (lax.rem(me + k, groups), lane))

    def row_copy(k):
        to = lax.rem(me + k, groups)
        return remote(returning.at[to], returned.at[me], row_sem, k, (to, lane))

    each(1, lanes, lambda k: lane_copy(scaled_ref, scaled_in, scaled_sem, k).start())
    each(1, outers, lambda k: pair_copy(k).start())
    pair_copy(0).start()
    each(1, lanes, lambda k: lane_copy(mixed_ref, mixed_in, mixed_sem, k).start())

    def pass_on(k):
        pair_copy(k).wait_recv()
        at = lax.rem(outer + k, outers)
        pair_sum[at] = (terms_ref[at * 2 + inner].astype(F32) + pair_in[at].astype(F32)).astype(BF16)
        outer_copy(k).start()

    pass_on(1)

    scaled_in[lane] = scaled_ref[:, span(lane, quarter)]
    each(1, lanes, lambda k: lane_copy(scaled_ref, scaled_in, scaled_sem, k).wait())
    share = scaled_in[0].astype(F32)
    for k in range(1, lanes):
        share = share + scaled_in[k].astype(F32)
    normed = normed_ref[...]
    grown = share * gain_ref[...]
    ones = jnp.ones((8, quarter), F32)
    sums_out[0:8, :] = dot(ones, grown, NT, lax.Precision.HIGHEST)
    sums_out[8:16, :] = dot(ones, grown * normed, NT, lax.Precision.HIGHEST)
    each(1, lanes, lambda k: sums_copy(k).start())
    small_out[...] = tap_ref[...]
    small_out[KSIZE:KSIZE + 1, :] = jnp.sum(share * normed, axis=0, keepdims=True)
    each(1, groups, lambda k: small_copy(k).start())
    each(2, outers, pass_on)
    pair_copy(0).wait_recv()
    own = terms_ref[me].astype(F32) + pair_in[outer].astype(F32)
    sums_in[lane] = sums_out[...]
    each(1, lanes, lambda k: sums_copy(k).wait())
    sums = sums_in[0]
    for k in range(1, lanes):
        sums = sums + sums_in[k]
    means = jnp.transpose(sums) * (1.0 / (lanes * quarter))
    back = inv_ref[...] * (grown - means[:, 0:1] - normed * means[:, 8:9]) + cot_ref[...].astype(F32)
    returning[...] = dot(place_ref[...], back.astype(BF16)).astype(BF16).reshape(groups, cap, quarter)
    each(1, groups, lambda k: row_copy(k).start())

    mixed_in[lane] = mixed_ref[:, span(lane, quarter)]
    each(1, lanes, lambda k: lane_copy(mixed_ref, mixed_in, mixed_sem, k).wait())
    mixed = mixed_in[0].astype(F32)
    for k in range(1, lanes):
        mixed = mixed + mixed_in[k].astype(F32)
    out_ref[...] = (local_ref[...].astype(F32) + mixed).astype(BF16)

    small_in[me] = small_out[...]
    each(1, groups, lambda k: small_copy(k).wait())
    small = small_in[0]
    for k in range(1, groups):
        small = small + small_in[k]
    small_ref[...] = small * scale

    returned[me] = returning[me]
    each(1, groups, lambda k: row_copy(k).wait())
    frames_ref[...] = dot(pick_ref[...], returned[...].reshape(slots, quarter), TN).astype(BF16)

    weight_ref[...] = own

    def add_up(k):
        outer_copy(k).wait_recv()
        weight_ref[...] += outer_in[lax.rem(outer - k + outers, outers)].astype(F32)

    each(1, outers, add_up)
    weight_ref[...] = weight_ref[...] * scale
    each(1, outers, lambda k: outer_copy(k).wait_send())
    each(0, outers, lambda k: pair_copy(k).wait_send())


def conv_masks(labels):
    length = labels.shape[0]
    padded = jnp.pad(labels, (HALF, HALF), constant_values=-1)
    return [
        (padded[k : k + length] == labels).astype(F32)[:, None] for k in range(KSIZE)
    ]


def shards(frames, owner_slot, segment, norm_gain, expand, kernel, project, cotangent):
    rows, quarter = frames.shape
    groups, lanes = lax.axis_size("dp"), lax.axis_size("seq")
    lane = lax.axis_index("seq")
    cap = max(16, rows // groups)
    slots = groups * cap
    depth = D // groups
    wide = 3 * quarter
    inv_root = 1.0 / math.sqrt(rows * groups)
    vmem = pl.BlockSpec(memory_space=pltpu.VMEM)
    anywhere = pl.BlockSpec(memory_space=pl.ANY)
    dma = pltpu.SemaphoreType.DMA
    weight = jnp.concatenate([expand.reshape(depth, 2 * quarter), project.T], axis=1)
    owner_rows = jnp.broadcast_to(owner_slot[None, :], (8, rows))
    local_rows, whole_rows, cot_full, weight_full, pick, place, total = pl.pallas_call(
        functools.partial(arrive_kernel, groups, lanes, cap),
        out_shape=(
            jax.ShapeDtypeStruct((rows, quarter), BF16),
            jax.ShapeDtypeStruct((rows, D), BF16),
            jax.ShapeDtypeStruct((rows, D), BF16),
            jax.ShapeDtypeStruct((groups, depth, wide), BF16),
            jax.ShapeDtypeStruct((slots, rows), BF16),
            jax.ShapeDtypeStruct((slots, rows), BF16),
            jax.ShapeDtypeStruct((8, 128), F32),
        ),
        in_specs=[vmem, vmem, anywhere, anywhere],
        out_specs=(vmem, anywhere, anywhere, anywhere, vmem, vmem, vmem),
        scratch_shapes=[
            pltpu.VMEM((groups, cap, quarter), BF16),
            pltpu.VMEM((groups, cap, quarter), BF16),
            pltpu.VMEM((groups, 8, rows), jnp.int32),
            dma((2, groups)), dma((2, groups)), dma((2, groups // 2)), dma((2, groups // 2)),
            dma((2, lanes)), dma((2, lanes)), dma((3,)),
        ],
        compiler_params=pltpu.CompilerParams(collective_id=0, has_side_effects=True, vmem_limit_bytes=40 << 20),
        name="arrive",
    )(owner_rows, frames, weight, cotangent)
    weight_full = weight_full.reshape(D, wide)
    expand_full = weight_full[:, : 2 * quarter]
    project_back = weight_full[:, 2 * quarter :]
    live_col = (lax.broadcasted_iota(jnp.int32, (rows, 1), 0).astype(F32) < total[0, 0]).astype(F32)
    floats = whole_rows.astype(F32)
    row_mean = jnp.mean(floats, axis=1, keepdims=True)
    centred = floats - row_mean
    inv_scale = lax.rsqrt(jnp.mean(centred * centred, axis=1, keepdims=True) + EPS)
    scaled = (centred * inv_scale * norm_gain).astype(BF16)
    normed_local = (local_rows.astype(F32) - row_mean) * inv_scale
    joined = dot(scaled, expand_full)
    value_half = joined[:, :quarter]
    gate_sig = jax.nn.sigmoid(joined[:, quarter:])
    glu_out = value_half * gate_sig
    masks = conv_masks(segment[0])
    around = jnp.pad(glu_out, ((HALF, HALF), (0, 0)))
    conv_out = sum(kernel[k] * around[k : k + rows] * masks[k] for k in range(KSIZE))
    conv_sig = jax.nn.sigmoid(conv_out)
    hidden = (conv_out * conv_sig * live_col).astype(BF16)
    mixed_part = dot(hidden, project_back, NT).astype(BF16)
    hidden_grad = dot(cot_full, project_back) * live_col
    conv_grad = hidden_grad * (conv_sig + conv_out * conv_sig * (1.0 - conv_sig))
    upstream = jnp.pad(conv_grad, ((HALF, HALF), (0, 0)))
    glu_grad = sum(
        kernel[k] * upstream[2 * HALF - k : 2 * HALF - k + rows] * masks[KSIZE - 1 - k] for k in range(KSIZE)
    )
    taps = jnp.stack(
        [jnp.sum(conv_grad * around[k : k + rows] * masks[k], axis=0) for k in range(KSIZE)]
    )
    proj_grad = jnp.concatenate(
        [glu_grad * gate_sig, glu_grad * value_half * gate_sig * (1.0 - gate_sig)], axis=1
    ).astype(BF16)
    terms = jnp.concatenate([dot(scaled, proj_grad, TN).astype(BF16), dot(cot_full, hidden, TN).astype(BF16)], axis=1)
    scaled_part = dot(proj_grad, expand_full, NT).astype(BF16)
    gain_local = lax.dynamic_slice_in_dim(norm_gain, lane * quarter, quarter, 0)[None, :]
    output, grad_frames, small, weight_grad = pl.pallas_call(
        functools.partial(leave_kernel, groups, lanes, cap, inv_root),
        out_shape=(
            jax.ShapeDtypeStruct((rows, quarter), BF16),
            jax.ShapeDtypeStruct((rows, quarter), BF16),
            jax.ShapeDtypeStruct((16, quarter), F32),
            jax.ShapeDtypeStruct((depth, wide), F32),
        ),
        in_specs=[vmem] * 11,
        out_specs=(vmem,) * 4,
        scratch_shapes=[
            pltpu.VMEM((groups // 2, depth, wide), BF16),
            pltpu.VMEM((groups // 2, depth, wide), BF16),
            pltpu.VMEM((groups // 2, depth, wide), BF16),
            pltpu.VMEM((lanes, rows, quarter), BF16),
            pltpu.VMEM((lanes, rows, quarter), BF16),
            pltpu.VMEM((groups, 16, quarter), F32),
            pltpu.VMEM((16, quarter), F32),
            pltpu.VMEM((lanes, 16, rows), F32),
            pltpu.VMEM((16, rows), F32),
            pltpu.VMEM((groups, cap, quarter), BF16),
            pltpu.VMEM((groups, cap, quarter), BF16),
            dma((2, groups // 2)), dma((2, groups // 2)), dma((2, lanes)), dma((2, lanes)),
            dma((2, groups)), dma((2, lanes)), dma((2, groups)),
        ],
        compiler_params=pltpu.CompilerParams(collective_id=1, has_side_effects=True, vmem_limit_bytes=48 << 20),
        name="leave",
    )(
        terms.reshape(groups, depth, wide), scaled_part, mixed_part, jnp.pad(taps, ((0, 16 - KSIZE), (0, 0))),
        cotangent, normed_local, inv_scale, gain_local, local_rows, pick, place,
    )
    return (
        output,
        grad_frames,
        small[KSIZE],
        small[:KSIZE],
        weight_grad[:, : 2 * quarter].reshape(depth, 2, quarter),
        weight_grad[:, 2 * quarter :].T,
    )


def solution(mesh):
    placed = (
        P("dp", "seq"),
        P("dp"),
        P("dp", None),
        P(),
        P("dp", None, "seq"),
        P(None, "seq"),
        P("seq", "dp"),
        P("dp", "seq"),
    )
    return jax.shard_map(
        shards,
        mesh=mesh,
        in_specs=placed,
        out_specs=(
            P("dp", "seq"),
            P("dp", "seq"),
            P("seq"),
            P(None, "seq"),
            P("dp", None, "seq"),
            P("seq", "dp"),
        ),
        check_vma=False,
    )
```

time: 526 us -> 189 us (0.36)
  waiting for transfers between devices: 382 us -> 0 us
  Pallas kernels: 0 us -> 144 us
  blocking collectives: 27.4 us -> 0 us
  starting transfers between devices: 16.5 us -> 0 us
  local copies, waits for them, and re-layouts: 36.4 us -> 20.6 us
  between operations: 15.4 us -> 1.05 us
  other arithmetic: 21 us -> 8.05 us
  matrix products: 22.8 us -> 13.5 us
    unnamed x10 -> x0, waiting for transfers between devices: 173 us -> none
    pallas_call x0 -> x2, Pallas kernels: none -> 144 us  [the longest x1 78.5 us: shards(): pl.pallas_call(functools.partial(leave_kernel, groups, lanes, cap, inv_ro...]
    all_gather x4 -> x0, waiting for transfers between devices: 127 us -> none  [the longest x1 50.4 us: shards(): lax.all_gather(expand, 'dp', axis=0, tiled=True).reshape(D, 2 * quarter)]
    reduce_scatter x1 -> x0, waiting for transfers between devices: 55.6 us -> none  [shards(): lax.psum_scatter(project_term, 'dp', scatter_dimension=1, tiled=True)]
    psum x1 -> x0, blocking collectives: 27.4 us -> none  [shards(): gain_sum, kernel_sum = lax.psum((gain_term, kernel_term), 'dp')]
    psum x1 -> x0, waiting for transfers between devices: 20.2 us -> none  [shards(): lax.psum(scaled_part.astype(jnp.bfloat16), 'seq').astype(jnp.float32)]
    all_to_all x3 -> x0, starting transfers between devices: 15.8 us -> none  [the longest x1 5.72 us: shards(): lax.all_to_all(landing_out, 'dp', split_axis=0, concat_axis=0, tiled=True)]
    gather x6 -> x0, local copies, waits for them, and re-layouts: 12.7 us -> none  [the longest x1 2.57 us: shards(): grad_frames = returned_flat[send_pos]]
  transfers between devices with their start and end apart: 11 -> 0, of which waited for: 9 -> 0; matrix products, arithmetic and copies ran while one was open for 9% -> 0% of each run, Pallas kernels for 0% -> 0%
where the time goes in v1:
time: 189 us; the launch traced here: 187 us
  Pallas kernels  144 us (76%)
  local copies, waits for them, and re-layouts  20.6 us (11%)
  matrix products  13.5 us (7%)
  other arithmetic  8.05 us (4%)
    pallas_call x1, Pallas kernels, shards(): pl.pallas_call(functools.partial(leave_kernel, groups, lanes, cap, inv_ro...  78.5 us
    pallas_call x1, Pallas kernels, shards(): pl.pallas_call(functools.partial(arrive_kernel, groups, lanes, cap), out_...  65.7 us
    dot_general x6, matrix products, dot(): lax.dot_general(a, b, dims, preferred_element_type=F32, precision=precision)  13.5 us
    unnamed x54, local copies, waits for them, and re-layouts  9.07 us
    concatenate x1, local copies, waits for them, and re-layouts, shards(): jnp.concatenate([dot(scaled, proj_grad, TN).astype(BF16), dot(cot_full, h...  5.79 us

profile of v1, /device:TPU:9, one launch (start us, length us, event | category | flops | bytes accessed | tf_op | source)
XLA Modules:
  0.0 187.5 jit_solution(11478617580314081124)
XLA Ops:
  1.3 1.0 copy.17
  2.3 0.9 pad_maximum_fusion.4.weight_ref
  3.3 1.0 copy-done
  4.3 1.0 copy-done.7
  5.3 65.7 %arrive.1 = (bf16[512,384]{1,0:T(8,128)(2,1)S(1)}, bf16[512,1536]{1,0:T(8,128)(2,1)S(1)}, bf16[512,1536]{1,0:T(8,128)(2,1)S(1)}, bf16[8,192,1152]{2,1,0:T(8,128)...) custom-call(s32[8,512]{1,0:T(8,128)S(1)} %broadcast_in_dim.4.owner_ref, ...), custom_call_target="tpu_custom_call" | custom-call | tf_op jit(solution)/shard_map/arrive/pallas_call | solution.py:284
  71.9 1.5 fusion.6
  75.0 1.3 multiply_add_fusion.1
  76.3 0.9 convolution_convert_fusion.3
  77.2 2.9 %multiply_reduce_fusion = (f32[384]{0:T(512)S(1)}, f32[384]{0:T(512)S(1)}, f32[384]{0:T(512)}, f32[384]{0:T(512)}, f32[384]{0:T(512)}, /*index=5*/f32[384]{0:T(5...) fusion(f32[512,384]{1,0:T(8,128)S(1)} %slice_multiply_fusion, f32[512]{0:T(512)S(1)} %get-tuple-element.55, ...), kind=kOutput, calls=%fused_computation.25 | convolution fusion | flops 610857600 | bytes 5144064 | tf_op jit(solution)/shard_map/dot_general | solution.py:22
  80.1 1.5 multiply_convert_fusion.2
  81.9 1.6 convolution_convert_fusion
  83.5 2.0 %pad_maximum_fusion = bf16[1536,1152]{0,1:T(8,128)(2,1)} fusion(bf16[1536,384]{0,1:T(8,128)(2,1)S(1)} %convolution_convert_fusion.3, bf16[1536,768]{0,1:T(8,128)(2,1)S(1)} %convolution_convert_fusion), kind=kLoop, calls=%fused_computation.4 | loop fusion | flops 7077888 | bytes 7077888 | tf_op jit(solution)/shard_map/concatenate | solution.py:339
  85.5 5.8 %copy.15 = bf16[1536,1152]{1,0:T(8,128)(2,1)} copy(bf16[1536,1152]{0,1:T(8,128)(2,1)} %pad_maximum_fusion) | data formatting | bytes 7077888 | tf_op jit(solution)/shard_map/concatenate | solution.py:339
  91.3 3.1 %convolution_convert_fusion.2.scaled_ref = bf16[512,1536]{1,0:T(8,128)(2,1)S(1)} fusion(bf16[1536,1152]{1,0:T(8,128)(2,1)} %bitcast.16, bf16[512,384]{1,0:T(8,128)(2,1)S(1)} %multiply_convert_fusion.1, bf16[512,384]{1,0:T(8,128)(2,1)S(1)} %get-tuple-element.46), kind=kOutput, calls=%fused_computation.10 | convolution fusion | flops 1210318848 | bytes 4718592 | tf_op jit(solution)/shard_map/dot_general | solution.py:22
  94.5 3.6 %convolution_convert_fusion.1.mixed_ref = bf16[512,1536]{1,0:T(8,128)(2,1)} fusion(bf16[1536,1152]{1,0:T(8,128)(2,1)} %bitcast.17, f32[512,384]{1,0:T(8,128)S(1)} %multiply_add_fusion.1, f32[512]{0:T(512)S(1)} %copy-done.23), kind=kOutput, calls=%fused_computation.9 | convolution fusion | flops 605945856 | bytes 3540992 | tf_op jit(solution)/shard_map/dot_general | solution.py:22
  98.6 0.8 dynamic_slice.3
  99.4 1.0 copy-done.4
  100.5 1.0 copy-done.6
  101.5 78.5 %leave.1 = (bf16[512,384]{1,0:T(8,128)(2,1)S(1)}, bf16[512,384]{1,0:T(8,128)(2,1)S(1)}, f32[16,384]{1,0:T(8,128)S(1)}, f32[192,1152]{1,0:T(8,128)S(1)}) custom-call(bf16[8,192,1152]{2,1,0:T(8,128)(2,1)} %bitcast.18, bf16[512,1536]{1,0:T(8,128)(2,1)S(1)} %convolution_convert_fusion.2.scaled_ref, bf16[512,1536]{1,0:T(8,128)(2,1)} %convolution_convert_fusion.1.mixed_ref, ...), custom_call_target="tpu_custom_call" | custom-call | tf_op jit(solution)/shard_map/leave/pallas_call | solution.py:342
  180.8 0.7 copy-done.10
  182.5 1.1 reshape.71
  183.7 1.7 slice_bitcast_fusion
  185.4 0.7 copy.21
  186.1 0.7 copy.22
  (72 shorter events, 6.2 us)
Async XLA Ops:
  3.3 1.0 copy-start
  4.3 1.0 copy-start.7
  5.3 66.6 %copy-start.24 = (f32[1536]{0:T(1024)S(1)}, f32[1536]{0:T(1024)}, u32[]{:S(2)}) copy-start(f32[1536]{0:T(1024)} %param.11) | copy-start | bytes 18436
  71.0 2.4 %copy-start.3 = (bf16[512,512]{1,0:T(8,128)(2,1)}, bf16[512,512]{1,0:T(8,128)(2,1)S(1)}, u32[]{:S(2)}) copy-start(bf16[512,512]{1,0:T(8,128)(2,1)S(1)} %get-tuple-element.22.pick_ref) | copy-start | bytes 1572868
  71.0 2.4 %copy-start.5 = (bf16[512,512]{1,0:T(8,128)(2,1)}, bf16[512,512]{1,0:T(8,128)(2,1)S(1)}, u32[]{:S(2)}) copy-start(bf16[512,512]{1,0:T(8,128)(2,1)S(1)} %get-tuple-element.23.place_ref) | copy-start | bytes 1572868
  71.0 6.2 %copy-start.12 = (bf16[8,192,1152]{2,1,0:T(8,128)(2,1)}, bf16[8,192,1152]{2,1,0:T(8,128)(2,1)S(1)}, u32[]{:S(2)}) copy-start(bf16[8,192,1152]{2,1,0:T(8,128)(2,1)S(1)} %get-tuple-element.19) | copy-start | bytes 10616836
  73.4 0.8 copy-start.21
  73.4 1.5 copy-start.13
  74.9 2.3 %copy-start.22 = (f32[512]{0:T(512)}, f32[512]{0:T(512)S(1)}, u32[]{:S(2)}) copy-start(f32[512]{0:T(512)S(1)} %get-tuple-element.57) | copy-start | bytes 6148
  91.3 3.1 %copy-start.23 = (f32[512]{0:T(512)S(1)}, f32[512]{0:T(512)}, u32[]{:S(2)}) copy-start(f32[512]{0:T(512)} %copy-done.22) | copy-start | bytes 6148
  94.4 3.7 %copy-start.20 = (f32[384]{0:T(512)S(1)}, f32[384]{0:T(512)}, u32[]{:S(2)}) copy-start(f32[384]{0:T(512)} %get-tuple-element.36) | copy-start | bytes 4612
  94.4 3.7 %copy-start.19 = (f32[384]{0:T(512)S(1)}, f32[384]{0:T(512)}, u32[]{:S(2)}) copy-start(f32[384]{0:T(512)} %get-tuple-element.35) | copy-start | bytes 4612
  94.4 3.7 %copy-start.18 = (f32[384]{0:T(512)S(1)}, f32[384]{0:T(512)}, u32[]{:S(2)}) copy-start(f32[384]{0:T(512)} %get-tuple-element.34) | copy-start | bytes 4612
  94.4 3.7 %copy-start.17 = (f32[384]{0:T(512)S(1)}, f32[384]{0:T(512)}, u32[]{:S(2)}) copy-start(f32[384]{0:T(512)} %get-tuple-element.33) | copy-start | bytes 4612
  94.4 3.7 %copy-start.16 = (f32[384]{0:T(512)S(1)}, f32[384]{0:T(512)}, u32[]{:S(2)}) copy-start(f32[384]{0:T(512)} %get-tuple-element.32) | copy-start | bytes 4612
  94.4 3.7 %copy-start.15 = (f32[384]{0:T(512)S(1)}, f32[384]{0:T(512)}, u32[]{:S(2)}) copy-start(f32[384]{0:T(512)} %get-tuple-element.31) | copy-start | bytes 4612
  94.5 3.7 %copy-start.14 = (f32[384]{0:T(512)S(1)}, f32[384]{0:T(512)}, u32[]{:S(2)}) copy-start(f32[384]{0:T(512)} %get-tuple-element.30) | copy-start | bytes 4612
  94.5 5.0 %copy-start.1 = (bf16[512,384]{1,0:T(8,128)(2,1)S(1)}, bf16[512,384]{1,0:T(8,128)(2,1)}, u32[]{:S(2)}) copy-start(bf16[512,384]{1,0:T(8,128)(2,1)} %cot_ref.3) | copy-start | bytes 1179652
  99.4 1.0 copy-start.4
  100.5 1.0 copy-start.6
  180.1 0.8 copy-start.8
  181.6 0.9 copy-start.2
  181.6 3.8 %copy-start.11 = (bf16[512,384]{1,0:T(8,128)(2,1)S(1)}, bf16[512,384]{1,0:T(8,128)(2,1)}, u32[]{:S(2)}) copy-start(bf16[512,384]{1,0:T(8,128)(2,1)} %copy-done.10) | copy-start | bytes 1179652
  181.6 4.5 %copy-start.9 = (bf16[512,384]{1,0:T(8,128)(2,1)S(1)}, bf16[512,384]{1,0:T(8,128)(2,1)}, u32[]{:S(2)}) copy-start(bf16[512,384]{1,0:T(8,128)(2,1)} %copy-done.8) | copy-start | bytes 1179652
  (1 other events, 0.7 us)

commit v2 on v1

v2 whole, which is shorter than its diff:
```python
import functools
import math

import jax
import jax.numpy as jnp
from jax import lax
from jax.experimental import pallas as pl
from jax.experimental.pallas import tpu as pltpu
from jax.sharding import PartitionSpec as P

D = 1536
KSIZE = 9
HALF = KSIZE // 2
EPS = 1e-05
BF16 = jnp.bfloat16
F32 = jnp.float32
NT = (((1,), (1,)), ((), ()))
TN = (((0,), (0,)), ((), ()))


def dot(a, b, dims=(((1,), (0,)), ((), ())), precision=None):
    return lax.dot_general(a, b, dims, preferred_element_type=F32, precision=precision)


def span(index, size):
    return pl.ds(pl.multiple_of(index * size, size), size)


def enter(groups, lanes):
    me, lane = lax.axis_index("dp"), lax.axis_index("seq")
    barrier = pltpu.get_barrier_semaphore()

    def greet_group(k, carry):
        pl.semaphore_signal(barrier, inc=1, device_id=(lax.rem(me + k, groups), lane),
                            device_id_type=pl.DeviceIdType.MESH)
        return carry

    def greet_lane(k, carry):
        pl.semaphore_signal(barrier, inc=1, device_id=(me, lax.rem(lane + k, lanes)),
                            device_id_type=pl.DeviceIdType.MESH)
        return carry

    lax.fori_loop(1, groups, greet_group, 0)
    lax.fori_loop(1, lanes, greet_lane, 0)
    pl.semaphore_wait(barrier, groups + lanes - 2)


def remote(src, dst, sems, k, device):
    return pltpu.make_async_remote_copy(
        src_ref=src, dst_ref=dst, send_sem=sems.at[0, k], recv_sem=sems.at[1, k],
        device_id=device, device_id_type=pl.DeviceIdType.MESH)


def each(first, last, body):
    def step(k, carry):
        body(k)
        return carry

    lax.fori_loop(first, last, step, 0)


def flat(parts):
    n, rows, columns = parts.shape
    if rows % 16:
        return parts.astype(F32).reshape(n * rows, columns).astype(BF16)
    return parts.reshape(n * rows, columns)


def sigmoid(x):
    return 1.0 / (1.0 + jnp.exp(-x))


def block_kernel(groups, lanes, cap, scale,
                 owner_ref, frames_ref, expand_ref, project_ref, cot_ref, gain_ref, gain_local_ref, taps_ref, mask_ref,
                 out_ref, back_ref, small_ref, grad_expand_ref, grad_project_ref,
                 outgoing, incoming, owners, pick, place, local, whole, cot_full, scaled, expand_full, project_full,
                 around, upstream, conv, value, gate, mixed_part, scaled_part,
                 expand_terms, expand_in, expand_sum, expand_last, project_terms, project_in, project_sum, project_last,
                 scaled_in, mixed_in, small_in, small_out, sums_in, sums_out, returning, returned,
                 owner_sem, row_sem, cot_sem, whole_sem, eo_sem, ep_sem, po_sem, pp_sem,
                 ge_pair, ge_outer, gp_pair, gp_outer, scaled_sem, mixed_sem, small_sem, sums_sem, back_sem):
    rows, quarter = frames_ref.shape
    depth = expand_ref.shape[0]
    me, lane = lax.axis_index("dp"), lax.axis_index("seq")
    outers = groups // 2
    outer, inner = me // 2, lax.rem(me, 2)
    mate = outer * 2 + 1 - inner
    high, low = lane // 2, lax.rem(lane, 2)
    sibling = high * 2 + 1 - low
    opposite = lax.rem(lane + 2, lanes)
    slots = groups * cap
    enter(groups, lanes)

    def to_group(src, dst, sems):
        def copy(k):
            return remote(src, dst.at[me], sems, k, (lax.rem(me + k, groups), lane))
        return copy

    def rows_to_group(src, dst, sems):
        def copy(k):
            to = lax.rem(me + k, groups)
            return remote(src.at[to], dst.at[me], sems, k, (to, lane))
        return copy

    def lane_gather(buffer, sems):
        own, far = buffer.at[:, span(lane, quarter)], buffer.at[:, span(opposite, quarter)]
        return (remote(own, own, sems, 0, (me, opposite)), remote(own, own, sems, 1, (me, sibling)),
                remote(far, far, sems, 2, (me, sibling)))

    def lane_scatter(src, dst, sems):
        def copy(k):
            to = lax.rem(lane + k, lanes)
            return remote(src.at[:, span(to, quarter)], dst.at[lane], sems, k, (me, to))
        return copy

    def gather_outer(full, sems):
        def copy(k):
            return remote(full.at[me], full.at[me], sems, k, (lax.rem(outer + k, outers) * 2 + inner, lane))
        return copy

    def gather_pair(full, sems):
        def copy(k):
            held = lax.rem(outer - k + outers, outers) * 2 + inner
            return remote(full.at[held], full.at[held], sems, k, (mate, lane))
        return copy

    def term_pair(terms, landing, sems):
        def copy(k):
            at = lax.rem(outer + k, outers)
            return remote(terms.at[at * 2 + 1 - inner], landing.at[at], sems, k, (mate, lane))
        return copy

    def term_outer(summed, landing, sems):
        def copy(k):
            at = lax.rem(outer + k, outers)
            return remote(summed.at[at], landing.at[outer], sems, k, (at * 2 + inner, lane))
        return copy

    owner_copy = to_group(owner_ref, owners, owner_sem)
    row_copy = rows_to_group(outgoing, incoming, row_sem)
    cot_copies = lane_gather(cot_full, cot_sem)
    whole_copies = lane_gather(whole, whole_sem)
    expand_outer, expand_pair = gather_outer(expand_full, eo_sem), gather_pair(expand_full, ep_sem)
    project_outer, project_pair = gather_outer(project_full, po_sem), gather_pair(project_full, pp_sem)
    mixed_copy = lane_scatter(mixed_part, mixed_in, mixed_sem)
    scaled_copy = lane_scatter(scaled_part, scaled_in, scaled_sem)
    gp_first, gp_second = term_pair(project_terms, project_in, gp_pair), term_outer(project_sum, project_last, gp_outer)
    ge_first, ge_second = term_pair(expand_terms, expand_in, ge_pair), term_outer(expand_sum, expand_last, ge_outer)
    small_copy = to_group(small_out, small_in, small_sem)
    back_copy = rows_to_group(returning, returned, back_sem)

    def sums_copy(k):
        return remote(sums_out, sums_in.at[lane], sums_sem, k, (me, lax.rem(lane + k, lanes)))

    each(1, groups, lambda k: owner_copy(k).start())
    slot = owner_ref[0:1, :]
    group_id = lax.broadcasted_iota(jnp.int32, (groups, rows), 0)
    named = jnp.where((slot >= group_id * rows) & (slot < group_id * rows + rows), 1.0, 0.0)
    before = jnp.where(lax.broadcasted_iota(jnp.int32, (rows, rows), 0)
                       < lax.broadcasted_iota(jnp.int32, (rows, rows), 1), 1.0, 0.0).astype(BF16)
    rank = dot(named.astype(BF16), before)
    position = jnp.sum((rank + group_id.astype(F32) * cap + 1.0) * named, axis=0, keepdims=True) - 1.0
    pick[...] = jnp.where(lax.broadcasted_iota(jnp.int32, (slots, rows), 0) == position.astype(jnp.int32), 1.0, 0.0).astype(BF16)
    outgoing[...] = dot(pick[...], frames_ref[...]).astype(BF16).reshape(groups, cap, quarter)
    each(1, groups, lambda k: row_copy(k).start())
    expand_full[me] = expand_ref[...]
    expand_pair(0).start()
    each(1, outers, lambda k: expand_outer(k).start())
    cot_full[:, span(lane, quarter)] = cot_ref[...]
    cot_copies[0].start()
    cot_copies[1].start()

    project_full[me] = project_ref[...]
    owners[me] = owner_ref[...]
    incoming[me] = outgoing[me]
    each(1, groups, lambda k: owner_copy(k).wait())
    mine = lax.broadcasted_iota(jnp.int32, (1, rows), 1) * 0 + me * rows
    total = jnp.zeros((1, 1), F32)
    row_id = lax.broadcasted_iota(jnp.int32, (cap, rows), 1).astype(F32)
    step_id = lax.broadcasted_iota(jnp.int32, (cap, rows), 0).astype(F32)
    for source in range(groups):
        theirs = owners[source][0:1, :]
        count = jnp.sum(jnp.where((theirs >= mine) & (theirs < mine + rows), 1.0, 0.0), axis=1, keepdims=True)
        hit = (row_id - step_id == total) & (step_id < count)
        place[pl.ds(source * cap, cap), :] = jnp.where(hit, 1.0, 0.0).astype(BF16)
        total = total + count
    live = jnp.where(lax.broadcasted_iota(jnp.int32, (rows, quarter), 0).astype(F32) < total, 1.0, 0.0)
    each(1, groups, lambda k: row_copy(k).wait())
    local[...] = dot(place[...], incoming[...].reshape(slots, quarter), TN).astype(BF16)
    whole[:, span(lane, quarter)] = local[...]
    whole_copies[0].start()
    whole_copies[1].start()
    cot_copies[0].wait_recv()
    cot_copies[2].start()
    whole_copies[0].wait_recv()
    whole_copies[2].start()

    def expand_on(k):
        expand_outer(k).wait_recv()
        expand_pair(k).start()

    each(1, outers, expand_on)
    project_pair(0).start()
    each(1, outers, lambda k: project_outer(k).start())

    for copies in (whole_copies,):
        copies[0].wait_send()
        copies[1].wait()
        copies[2].wait()
    floats = whole[...].astype(F32)
    row_mean = jnp.mean(floats, axis=1, keepdims=True)
    centred = floats - row_mean
    inv_scale = lax.rsqrt(jnp.mean(centred * centred, axis=1, keepdims=True) + EPS)
    scaled[...] = (centred * inv_scale * gain_ref[...]).astype(BF16)

    each(1, outers, lambda k: expand_outer(k).wait_send())
    each(0, outers, lambda k: expand_pair(k).wait())
    expand = flat(expand_full[...])
    joined = dot(scaled[...], expand)
    value[...] = joined[:, :quarter]
    gate[...] = sigmoid(joined[:, quarter:])

    def project_on(k):
        project_outer(k).wait_recv()
        project_pair(k).start()

    each(1, outers, project_on)
    edge = jnp.zeros((8, quarter), F32)
    around[0:8, :] = edge
    around[8 + rows:16 + rows, :] = edge
    around[8:8 + rows, :] = value[...] * gate[...]
    total_conv = jnp.zeros((rows, quarter), F32)
    for k in range(KSIZE):
        total_conv += taps_ref[k:k + 1, :] * around[8 - HALF + k:8 - HALF + k + rows, :] * mask_ref[:, k:k + 1]
    conv[...] = total_conv
    conv_sig = sigmoid(total_conv)
    hidden = (total_conv * conv_sig * live).astype(BF16)
    cot_copies[0].wait_send()
    cot_copies[1].wait()
    cot_copies[2].wait()
    project_terms[...] = dot(cot_full[...], hidden, TN).reshape(groups, depth, quarter).astype(BF16)
    each(1, outers, lambda k: gp_first(k).start())
    gp_first(0).start()

    each(1, outers, lambda k: project_outer(k).wait_send())
    each(0, outers, lambda k: project_pair(k).wait())
    project_back = flat(project_full[...])
    mixed_part[...] = dot(hidden, project_back, NT).astype(BF16)
    each(1, lanes, lambda k: mixed_copy(k).start())
    hidden_grad = dot(cot_full[...], project_back) * live
    conv_out = conv[...]
    conv_sig = sigmoid(conv_out)
    upstream[0:8, :] = edge
    upstream[8 + rows:16 + rows, :] = edge
    upstream[8:8 + rows, :] = hidden_grad * (conv_sig + conv_out * conv_sig * (1.0 - conv_sig))
    glu_grad = jnp.zeros((rows, quarter), F32)
    for k in range(KSIZE):
        glu_grad += (taps_ref[k:k + 1, :] * upstream[8 + HALF - k:8 + HALF - k + rows, :]
                     * mask_ref[:, KSIZE - 1 - k:KSIZE - k])
    gate_sig = gate[...]
    near = glu_grad * gate_sig
    proj_grad = jnp.concatenate([near.astype(BF16), (near * value[...] * (1.0 - gate_sig)).astype(BF16)], axis=1)
    expand_terms[...] = dot(scaled[...], proj_grad, TN).reshape(groups, depth, 2 * quarter).astype(BF16)
    each(1, outers, lambda k: ge_first(k).start())
    ge_first(0).start()
    scaled_part[...] = dot(proj_grad, expand, NT).astype(BF16)
    each(1, lanes, lambda k: scaled_copy(k).start())

    def project_term_on(k):
        gp_first(k).wait_recv()
        at = lax.rem(outer + k, outers)
        project_sum[at] = (project_terms[at * 2 + inner].astype(F32) + project_in[at].astype(F32)).astype(BF16)
        gp_second(k).start()

    def expand_term_on(k):
        ge_first(k).wait_recv()
        at = lax.rem(outer + k, outers)
        expand_sum[at] = (expand_terms[at * 2 + inner].astype(F32) + expand_in[at].astype(F32)).astype(BF16)
        ge_second(k).start()

    each(1, outers, project_term_on)
    small_out[...] = jnp.zeros(small_out.shape, F32)
    for k in range(KSIZE):
        small_out[k:k + 1, :] = jnp.sum(
            upstream[8:8 + rows, :] * around[8 - HALF + k:8 - HALF + k + rows, :] * mask_ref[:, k:k + 1],
            axis=0, keepdims=True)
    gp_first(0).wait_recv()
    grad_project_ref[...] = project_terms[me].astype(F32) + project_in[outer].astype(F32)
    expand_term_on(1)

    mixed_in[lane] = mixed_part[:, span(lane, quarter)]
    each(1, lanes, lambda k: mixed_copy(k).wait())
    mixed = mixed_in[0].astype(F32)
    for k in range(1, lanes):
        mixed = mixed + mixed_in[k].astype(F32)
    out_ref[...] = (local[...].astype(F32) + mixed).astype(BF16)

    scaled_in[lane] = scaled_part[:, span(lane, quarter)]
    each(1, lanes, lambda k: scaled_copy(k).wait())
    share = scaled_in[0].astype(F32)
    for k in range(1, lanes):
        share = share + scaled_in[k].astype(F32)
    normed = (local[...].astype(F32) - row_mean) * inv_scale
    grown = share * gain_local_ref[...]
    ones = jnp.ones((8, quarter), F32)
    sums_out[0:8, :] = dot(ones, grown, NT, lax.Precision.HIGHEST)
    sums_out[8:16, :] = dot(ones, grown * normed, NT, lax.Precision.HIGHEST)
    each(1, lanes, lambda k: sums_copy(k).start())
    small_out[KSIZE:KSIZE + 1, :] = jnp.sum(share * normed, axis=0, keepdims=True)
    each(1, groups, lambda k: small_copy(k).start())
    if outers > 2:
        expand_term_on(2)
    sums_in[lane] = sums_out[...]
    each(1, lanes, lambda k: sums_copy(k).wait())
    sums = sums_in[0]
    for k in range(1, lanes):
        sums = sums + sums_in[k]
    means = jnp.transpose(sums) * (1.0 / (lanes * quarter))
    back = inv_scale * (grown - means[:, 0:1] - normed * means[:, 8:9]) + cot_ref[...].astype(F32)
    returning[...] = dot(place[...], back.astype(BF16)).astype(BF16).reshape(groups, cap, quarter)
    each(1, groups, lambda k: back_copy(k).start())
    each(3, outers, expand_term_on)
    ge_first(0).wait_recv()
    grad_expand_ref[...] = expand_terms[me].astype(F32) + expand_in[outer].astype(F32)

    def project_add(k):
        gp_second(k).wait_recv()
        grad_project_ref[...] += project_last[lax.rem(outer - k + outers, outers)].astype(F32)

    each(1, outers, project_add)
    grad_project_ref[...] = grad_project_ref[...] * scale

    small_in[me] = small_out[...]
    each(1, groups, lambda k: small_copy(k).wait())
    small = small_in[0]
    for k in range(1, groups):
        small = small + small_in[k]
    small_ref[...] = small * scale

    returned[me] = returning[me]
    each(1, groups, lambda k: back_copy(k).wait())
    back_ref[...] = dot(pick[...], returned[...].reshape(slots, quarter), TN).astype(BF16)

    def expand_add(k):
        ge_second(k).wait_recv()
        grad_expand_ref[...] += expand_last[lax.rem(outer - k + outers, outers)].astype(F32)

    each(1, outers, expand_add)
    grad_expand_ref[...] = grad_expand_ref[...] * scale
    each(1, outers, lambda k: gp_second(k).wait_send())
    each(1, outers, lambda k: ge_second(k).wait_send())
    each(0, outers, lambda k: gp_first(k).wait_send())
    each(0, outers, lambda k: ge_first(k).wait_send())


def shards(frames, owner_slot, segment, norm_gain, expand, kernel, project, cotangent):
    rows, quarter = frames.shape
    groups, lanes = lax.axis_size("dp"), lax.axis_size("seq")
    lane = lax.axis_index("seq")
    cap = max(16, rows // groups)
    slots = groups * cap
    depth = D // groups
    outers = groups // 2
    inv_root = 1.0 / math.sqrt(rows * groups)
    vmem = pl.BlockSpec(memory_space=pltpu.VMEM)

    def sems(count):
        return pltpu.SemaphoreType.DMA((2, count))

    def terms(count, columns):
        return pltpu.VMEM((count, depth, columns), BF16)

    owner_rows = jnp.broadcast_to(owner_slot[None, :], (8, rows))
    labels = jnp.pad(segment[0], (HALF, HALF), constant_values=-1)
    masks = jnp.stack(
        [(labels[k : k + rows] == segment[0]).astype(F32) for k in range(KSIZE)] + [jnp.zeros((rows,), F32)] * (16 - KSIZE),
        axis=1,
    )
    gain_local = lax.dynamic_slice_in_dim(norm_gain, lane * quarter, quarter, 0)[None, :]
    share = pltpu.VMEM((rows, quarter), F32)
    padded = pltpu.VMEM((rows + 16, quarter), F32)
    all_columns = pltpu.VMEM((rows, D), BF16)
    buckets = pltpu.VMEM((groups, cap, quarter), BF16)
    lane_parts = pltpu.VMEM((lanes, rows, quarter), BF16)
    choice = pltpu.VMEM((slots, rows), BF16)
    output, grad_frames, small, grad_expand, grad_project = pl.pallas_call(
        functools.partial(block_kernel, groups, lanes, cap, inv_root),
        out_shape=(
            jax.ShapeDtypeStruct((rows, quarter), BF16),
            jax.ShapeDtypeStruct((rows, quarter), BF16),
            jax.ShapeDtypeStruct((16, quarter), F32),
            jax.ShapeDtypeStruct((depth, 2 * quarter), F32),
            jax.ShapeDtypeStruct((depth, quarter), F32),
        ),
        in_specs=[vmem] * 9,
        out_specs=(vmem,) * 5,
        scratch_shapes=[
            buckets, buckets, pltpu.VMEM((groups, 8, rows), jnp.int32), choice, choice,
            pltpu.VMEM((rows, quarter), BF16), all_columns, all_columns, all_columns,
            terms(groups, 2 * quarter), terms(groups, quarter),
            padded, padded, share, share, share, all_columns, all_columns,
            terms(groups, 2 * quarter), terms(outers, 2 * quarter), terms(outers, 2 * quarter), terms(outers, 2 * quarter),
            terms(groups, quarter), terms(outers, quarter), terms(outers, quarter), terms(outers, quarter),
            lane_parts, lane_parts,
            pltpu.VMEM((groups, 16, quarter), F32), pltpu.VMEM((16, quarter), F32),
            pltpu.VMEM((lanes, 16, rows), F32), pltpu.VMEM((16, rows), F32),
            buckets, buckets,
            sems(groups), sems(groups), sems(lanes), sems(lanes),
            sems(outers), sems(outers), sems(outers), sems(outers),
            sems(outers), sems(outers), sems(outers), sems(outers),
            sems(lanes), sems(lanes), sems(groups), sems(lanes), sems(groups),
        ],
        compiler_params=pltpu.CompilerParams(collective_id=0, has_side_effects=True, vmem_limit_bytes=58 << 20),
        name="conv_block",
    )(
        owner_rows, frames, expand.reshape(depth, 2 * quarter), project.T, cotangent,
        norm_gain[None, :], gain_local, kernel, masks,
    )
    return (
        output,
        grad_frames,
        small[KSIZE],
        small[:KSIZE],
        grad_expand.reshape(depth, 2, quarter),
        grad_project.T,
    )


def solution(mesh):
    placed = (
        P("dp", "seq"),
        P("dp"),
        P("dp", None),
        P(),
        P("dp", None, "seq"),
        P(None, "seq"),
        P("seq", "dp"),
        P("dp", "seq"),
    )
    return jax.shard_map(
        shards,
        mesh=mesh,
        in_specs=placed,
        out_specs=(
            P("dp", "seq"),
            P("dp", "seq"),
            P("seq"),
            P(None, "seq"),
            P("dp", None, "seq"),
            P("seq", "dp"),
        ),
        check_vma=False,
    )
```

time: 189 us -> 157 us (0.83)
  matrix products: 13.5 us -> 0 us
  local copies, waits for them, and re-layouts: 20.6 us -> 12.4 us
  other arithmetic: 8.05 us -> 1.09 us
  Pallas kernels: 144 us -> 142 us
    dot_general x6 -> x0, matrix products: 13.5 us -> none  [dot(): lax.dot_general(a, b, dims, preferred_element_type=F32, precision=precision)]
    concatenate x1 -> x0, local copies, waits for them, and re-layouts: 5.79 us -> none  [shards(): jnp.concatenate([dot(scaled, proj_grad, TN).astype(BF16), dot(cot_full, h...]
    unnamed x54 -> x15, local copies, waits for them, and re-layouts: 9.07 us -> 3.97 us
    concatenate x2 -> x0, other arithmetic: 3 us -> none  [the longest x1 2.05 us: shards(): jnp.concatenate([dot(scaled, proj_grad, TN).astype(BF16), dot(cot_full, h...]
    pallas_call x2 -> x1, Pallas kernels: 144 us -> 142 us  [shards(): pl.pallas_call(functools.partial(block_kernel, groups, lanes, cap, inv_ro...]
where the time goes in v2:
time: 157 us
  Pallas kernels  142 us (90%)
  local copies, waits for them, and re-layouts  12.4 us (8%)
    pallas_call x1, Pallas kernels, shards(): pl.pallas_call(functools.partial(block_kernel, groups, lanes, cap, inv_ro...  142 us
    unnamed x15, local copies, waits for them, and re-layouts  3.97 us

profile of v2, /device:TPU:9, one launch (start us, length us, event | category | flops | bytes accessed | tf_op | source)
XLA Modules:
  0.0 156.6 jit_solution(14149354014287012010)
XLA Ops:
  0.6 0.0 copy-start.2
  0.6 0.8 dynamic_slice.3
  1.5 0.6 broadcast_in_dim.14.gain_local_ref
  2.0 1.3 broadcast_in_dim.13.gain_ref
  3.3 1.3 broadcast_in_dim.12.owner_ref
  4.6 1.1 fusion.8
  5.7 0.1 stack.76
  5.8 0.8 copy.22.mask_ref
  6.7 0.0 copy-done.2
  6.7 0.7 copy.23
  7.4 142.4 %conv_block.1 = (bf16[512,384]{1,0:T(8,128)(2,1)}, bf16[512,384]{1,0:T(8,128)(2,1)}, f32[16,384]{1,0:T(8,128)}, f32[192,768]{1,0:T(8,128)}, f32[192,384]{1,0:T(8,128)}) custom-call(s32[8,512]{1,0:T(8,128)} %broadcast_in_dim.12.owner_ref, bf16[512,384]{1,0:T(8,128)(2,1)} %frames_ref.1, bf16[192,768]{1,0:T(8,128)(2,1)} %bitcast.14, bf16[192,384]{1,0:T(8,128)(2,1)} %bitcast.17, ...), custom_call_target="tpu_custom_call" | custom-call | tf_op jit(solution)/shard_map/conv_block/pallas_call | solution.py:386
  149.8 1.3 slice_reduce_fusion
  151.1 0.0 copy-start.1
  151.2 2.2 %reshape.20 = f32[192,2,384]{2,1,0:T(2,128)} reshape(f32[192,768]{1,0:T(8,128)} %get-tuple-element.14) | data formatting | bytes 1179648 | tf_op jit(solution)/shard_map/reshape | solution.py:424
  153.4 0.0 copy-done.1
  153.4 0.0 copy-start
  153.4 0.7 copy.28
  154.1 0.4 copy-done
  154.5 0.0 copy-start.4
  154.5 0.7 copy.29
  155.3 0.0 copy-done.4
  155.3 0.6 copy.30
  155.9 0.0 copy-done.3
  155.9 0.7 copy.31
  (5 shorter events, 0.0 us)
Async XLA Ops:
  0.6 6.0 %copy-start.2 = (bf16[192,2,384]{2,1,0:T(2,128)(2,1)S(1)}, bf16[192,2,384]{2,1,0:T(2,128)(2,1)}, u32[]{:S(2)}) copy-start(bf16[192,2,384]{2,1,0:T(2,128)(2,1)} %param.12) | copy-start | bytes 884740
  151.1 2.2 %copy-start.1 = (bf16[512,384]{1,0:T(8,128)(2,1)S(1)}, bf16[512,384]{1,0:T(8,128)(2,1)}, u32[]{:S(2)}) copy-start(bf16[512,384]{1,0:T(8,128)(2,1)} %get-tuple-element.30) | copy-start | bytes 1179652
  153.4 1.1 copy-start
  154.5 0.8 copy-start.4
  154.5 1.4 copy-start.3

commit v3 on v2

v3 whole, which is shorter than its diff:
```python
import functools
import math

import jax
import jax.numpy as jnp
from jax import lax
from jax.experimental import pallas as pl
from jax.experimental.pallas import tpu as pltpu
from jax.sharding import PartitionSpec as P

D = 1536
KSIZE = 9
HALF = KSIZE // 2
EPS = 1e-05
BF16 = jnp.bfloat16
F32 = jnp.float32
NT = (((1,), (1,)), ((), ()))
TN = (((0,), (0,)), ((), ()))


def dot(a, b, dims=(((1,), (0,)), ((), ())), precision=None):
    return lax.dot_general(a, b, dims, preferred_element_type=F32, precision=precision)


def span(index, size):
    return pl.ds(pl.multiple_of(index * size, size), size)


def enter(groups, lanes):
    me, lane = lax.axis_index("dp"), lax.axis_index("seq")
    barrier = pltpu.get_barrier_semaphore()

    def greet_group(k, carry):
        pl.semaphore_signal(barrier, inc=1, device_id=(lax.rem(me + k, groups), lane),
                            device_id_type=pl.DeviceIdType.MESH)
        return carry

    def greet_lane(k, carry):
        pl.semaphore_signal(barrier, inc=1, device_id=(me, lax.rem(lane + k, lanes)),
                            device_id_type=pl.DeviceIdType.MESH)
        return carry

    lax.fori_loop(1, groups, greet_group, 0)
    lax.fori_loop(1, lanes, greet_lane, 0)
    pl.semaphore_wait(barrier, groups + lanes - 2)


def remote(src, dst, sems, k, device):
    return pltpu.make_async_remote_copy(
        src_ref=src, dst_ref=dst, send_sem=sems.at[0, k], recv_sem=sems.at[1, k],
        device_id=device, device_id_type=pl.DeviceIdType.MESH)


def each(first, last, body):
    def step(k, carry):
        body(k)
        return carry

    lax.fori_loop(first, last, step, 0)


def flat(parts):
    n, rows, columns = parts.shape
    if rows % 16:
        return parts.astype(F32).reshape(n * rows, columns).astype(BF16)
    return parts.reshape(n * rows, columns)


def sigmoid(x):
    return 1.0 / (1.0 + jnp.exp(-x))


def block_kernel(groups, lanes, cap, scale,
                 owner_ref, segment_ref, frames_ref, expand_ref, project_ref, cot_ref, gain_ref, taps_ref,
                 out_ref, back_ref, small_ref, grad_expand_ref, grad_project_ref,
                 owner_out, labels, outgoing, incoming, owners, pick, place, local, whole, cot_full, scaled, weights,
                 around, upstream, conv, value, gate, mixed_part, scaled_part,
                 terms, terms_in, terms_sum, terms_last,
                 scaled_in, mixed_in, small_in, small_out, sums_in, sums_out, returning, returned,
                 owner_sem, row_sem, cot_sem, whole_sem, gather_outer_sem, gather_pair_sem,
                 term_pair_sem, term_outer_sem, scaled_sem, mixed_sem, small_sem, sums_sem, back_sem):
    rows, quarter = frames_ref.shape
    depth = expand_ref.shape[1]
    me, lane = lax.axis_index("dp"), lax.axis_index("seq")
    outers = groups // 2
    outer, inner = me // 2, lax.rem(me, 2)
    mate = outer * 2 + 1 - inner
    high, low = lane // 2, lax.rem(lane, 2)
    sibling = high * 2 + 1 - low
    opposite = lax.rem(lane + 2, lanes)
    slots = groups * cap
    owner_out[...] = jnp.broadcast_to(owner_ref[...], owner_out.shape)
    enter(groups, lanes)

    def to_group(src, dst, sems):
        def copy(k):
            return remote(src, dst.at[me], sems, k, (lax.rem(me + k, groups), lane))
        return copy

    def rows_to_group(src, dst, sems):
        def copy(k):
            to = lax.rem(me + k, groups)
            return remote(src.at[to], dst.at[me], sems, k, (to, lane))
        return copy

    def lane_gather(buffer, sems):
        own, far = buffer.at[:, span(lane, quarter)], buffer.at[:, span(opposite, quarter)]
        return (remote(own, own, sems, 0, (me, opposite)), remote(own, own, sems, 1, (me, sibling)),
                remote(far, far, sems, 2, (me, sibling)))

    def lane_scatter(src, dst, sems):
        def copy(k):
            to = lax.rem(lane + k, lanes)
            return remote(src.at[:, span(to, quarter)], dst.at[lane], sems, k, (me, to))
        return copy

    def gather_outer(u, k):
        part = weights.at[u, me]
        return remote(part, part, gather_outer_sem, u * outers + k, (lax.rem(outer + k, outers) * 2 + inner, lane))

    def gather_pair(u, k):
        part = weights.at[u, lax.rem(outer - k + outers, outers) * 2 + inner]
        return remote(part, part, gather_pair_sem, u * outers + k, (mate, lane))

    def term_pair(u, k):
        at = lax.rem(outer + k, outers)
        return remote(terms.at[u, at * 2 + 1 - inner], terms_in.at[u, at], term_pair_sem, u * outers + k, (mate, lane))

    def term_outer(u, k):
        at = lax.rem(outer + k, outers)
        return remote(terms_sum.at[u, at], terms_last.at[u, outer], term_outer_sem, u * outers + k,
                      (at * 2 + inner, lane))

    def gather_start(u):
        gather_pair(u, 0).start()
        each(1, outers, lambda k: gather_outer(u, k).start())

    def gather_on(u):
        def step(k):
            gather_outer(u, k).wait_recv()
            gather_pair(u, k).start()

        each(1, outers, step)

    def gather_end(u):
        each(1, outers, lambda k: gather_outer(u, k).wait_send())
        each(0, outers, lambda k: gather_pair(u, k).wait())

    def term_start(u, product):
        terms[u] = product.reshape(groups, depth, quarter).astype(BF16)
        each(1, outers, lambda k: term_pair(u, k).start())
        term_pair(u, 0).start()

    def term_on(u):
        def step(k):
            term_pair(u, k).wait_recv()
            at = lax.rem(outer + k, outers)
            terms_sum[u, at] = (terms[u, at * 2 + inner].astype(F32) + terms_in[u, at].astype(F32)).astype(BF16)
            term_outer(u, k).start()

        each(1, outers, step)
        term_pair(u, 0).wait_recv()

    def term_end(u):
        def step(k, total):
            term_outer(u, k).wait_recv()
            return total + terms_last[u, lax.rem(outer - k + outers, outers)].astype(F32)

        own = terms[u, me].astype(F32) + terms_in[u, outer].astype(F32)
        return lax.fori_loop(1, outers, step, own) * scale

    owner_copy = to_group(owner_out, owners, owner_sem)
    row_copy = rows_to_group(outgoing, incoming, row_sem)
    cot_copies = lane_gather(cot_full, cot_sem)
    whole_copies = lane_gather(whole, whole_sem)
    mixed_copy = lane_scatter(mixed_part, mixed_in, mixed_sem)
    scaled_copy = lane_scatter(scaled_part, scaled_in, scaled_sem)
    small_copy = to_group(small_out, small_in, small_sem)
    back_copy = rows_to_group(returning, returned, back_sem)

    def sums_copy(k):
        return remote(sums_out, sums_in.at[lane], sums_sem, k, (me, lax.rem(lane + k, lanes)))

    each(1, groups, lambda k: owner_copy(k).start())
    weights[0, me] = expand_ref[0]
    weights[1, me] = expand_ref[1]
    weights[2, me] = project_ref[...]
    gather_start(0)
    slot = owner_ref[0:1, :]
    group_id = lax.broadcasted_iota(jnp.int32, (groups, rows), 0)
    named = jnp.where((slot >= group_id * rows) & (slot < group_id * rows + rows), 1.0, 0.0)
    before = jnp.where(lax.broadcasted_iota(jnp.int32, (rows, rows), 0)
                       < lax.broadcasted_iota(jnp.int32, (rows, rows), 1), 1.0, 0.0).astype(BF16)
    rank = dot(named.astype(BF16), before)
    position = jnp.sum((rank + group_id.astype(F32) * cap + 1.0) * named, axis=0, keepdims=True) - 1.0
    pick[...] = jnp.where(lax.broadcasted_iota(jnp.int32, (slots, rows), 0) == position.astype(jnp.int32), 1.0, 0.0).astype(BF16)
    outgoing[...] = dot(pick[...], frames_ref[...]).astype(BF16).reshape(groups, cap, quarter)
    each(1, groups, lambda k: row_copy(k).start())
    gather_start(1)
    cot_full[:, span(lane, quarter)] = cot_ref[...]
    cot_copies[0].start()
    cot_copies[1].start()

    labels[0:8, :] = jnp.full((8, 128), -1.0, F32)
    labels[8 + rows:16 + rows, :] = jnp.full((8, 128), -1.0, F32)
    labels[8:8 + rows, :] = jnp.transpose(jnp.broadcast_to(segment_ref[...].astype(F32), (128, rows)))

    def mask(k):
        same = jnp.where(labels[8 - HALF + k:8 - HALF + k + rows, :] == labels[8:8 + rows, :], 1.0, 0.0)
        return jnp.concatenate([same] * (quarter // 128), axis=1)

    owners[me] = owner_out[...]
    incoming[me] = outgoing[me]
    each(1, groups, lambda k: owner_copy(k).wait())
    mine = lax.broadcasted_iota(jnp.int32, (1, rows), 1) * 0 + me * rows
    total = jnp.zeros((1, 1), F32)
    row_id = lax.broadcasted_iota(jnp.int32, (cap, rows), 1).astype(F32)
    step_id = lax.broadcasted_iota(jnp.int32, (cap, rows), 0).astype(F32)
    for source in range(groups):
        theirs = owners[source][0:1, :]
        count = jnp.sum(jnp.where((theirs >= mine) & (theirs < mine + rows), 1.0, 0.0), axis=1, keepdims=True)
        hit = (row_id - step_id == total) & (step_id < count)
        place[pl.ds(source * cap, cap), :] = jnp.where(hit, 1.0, 0.0).astype(BF16)
        total = total + count
    live = jnp.where(lax.broadcasted_iota(jnp.int32, (rows, quarter), 0).astype(F32) < total, 1.0, 0.0)
    gather_on(0)
    each(1, groups, lambda k: row_copy(k).wait())
    local[...] = dot(place[...], incoming[...].reshape(slots, quarter), TN).astype(BF16)
    whole[:, span(lane, quarter)] = local[...]
    whole_copies[0].start()
    whole_copies[1].start()
    gather_on(1)
    gather_start(2)
    whole_copies[0].wait_recv()
    whole_copies[2].start()
    cot_copies[0].wait_recv()
    cot_copies[2].start()
    for copies in (whole_copies,):
        copies[0].wait_send()
        copies[1].wait()
        copies[2].wait()
    floats = whole[...].astype(F32)
    row_mean = jnp.mean(floats, axis=1, keepdims=True)
    centred = floats - row_mean
    inv_scale = lax.rsqrt(jnp.mean(centred * centred, axis=1, keepdims=True) + EPS)
    scaled[...] = (centred * inv_scale * gain_ref[...]).astype(BF16)

    gather_end(0)
    expand_value = flat(weights[0])
    value[...] = dot(scaled[...], expand_value)
    gather_end(1)
    expand_gate = flat(weights[1])
    gate[...] = sigmoid(dot(scaled[...], expand_gate))
    gather_on(2)
    edge = jnp.zeros((8, quarter), F32)
    around[0:8, :] = edge
    around[8 + rows:16 + rows, :] = edge
    around[8:8 + rows, :] = value[...] * gate[...]
    total_conv = jnp.zeros((rows, quarter), F32)
    for k in range(KSIZE):
        total_conv += taps_ref[k:k + 1, :] * around[8 - HALF + k:8 - HALF + k + rows, :] * mask(k)
    conv[...] = total_conv
    conv_sig = sigmoid(total_conv)
    hidden = (total_conv * conv_sig * live).astype(BF16)
    cot_copies[0].wait_send()
    cot_copies[1].wait()
    cot_copies[2].wait()
    term_start(2, dot(cot_full[...], hidden, TN))
    gather_end(2)
    project_back = flat(weights[2])
    hidden_grad = dot(cot_full[...], project_back) * live
    conv_out = conv[...]
    conv_sig = sigmoid(conv_out)
    upstream[0:8, :] = edge
    upstream[8 + rows:16 + rows, :] = edge
    upstream[8:8 + rows, :] = hidden_grad * (conv_sig + conv_out * conv_sig * (1.0 - conv_sig))
    glu_grad = jnp.zeros((rows, quarter), F32)
    for k in range(KSIZE):
        glu_grad += (taps_ref[k:k + 1, :] * upstream[8 + HALF - k:8 + HALF - k + rows, :] * mask(KSIZE - 1 - k))
    gate_sig = gate[...]
    near = glu_grad * gate_sig
    value_grad = near.astype(BF16)
    gate_grad = (near * value[...] * (1.0 - gate_sig)).astype(BF16)
    term_start(0, dot(scaled[...], value_grad, TN))
    scaled_part[...] = (dot(value_grad, expand_value, NT) + dot(gate_grad, expand_gate, NT)).astype(BF16)
    each(1, lanes, lambda k: scaled_copy(k).start())
    term_start(1, dot(scaled[...], gate_grad, TN))
    term_on(2)
    mixed_part[...] = dot(hidden, project_back, NT).astype(BF16)
    each(1, lanes, lambda k: mixed_copy(k).start())
    small_out[...] = jnp.zeros(small_out.shape, F32)
    for k in range(KSIZE):
        small_out[k:k + 1, :] = jnp.sum(
            upstream[8:8 + rows, :] * around[8 - HALF + k:8 - HALF + k + rows, :] * mask(k),
            axis=0, keepdims=True)
    term_on(0)
    scaled_in[lane] = scaled_part[:, span(lane, quarter)]
    each(1, lanes, lambda k: scaled_copy(k).wait())
    share = scaled_in[0].astype(F32)
    for k in range(1, lanes):
        share = share + scaled_in[k].astype(F32)
    normed = (local[...].astype(F32) - row_mean) * inv_scale
    grown = share * gain_ref[:, span(lane, quarter)]
    ones = jnp.ones((8, quarter), F32)
    sums_out[0:8, :] = dot(ones, grown, NT, lax.Precision.HIGHEST)
    sums_out[8:16, :] = dot(ones, grown * normed, NT, lax.Precision.HIGHEST)
    each(1, lanes, lambda k: sums_copy(k).start())
    small_out[KSIZE:KSIZE + 1, :] = jnp.sum(share * normed, axis=0, keepdims=True)
    each(1, groups, lambda k: small_copy(k).start())
    sums_in[lane] = sums_out[...]
    each(1, lanes, lambda k: sums_copy(k).wait())
    sums = sums_in[0]
    for k in range(1, lanes):
        sums = sums + sums_in[k]
    means = jnp.transpose(sums) * (1.0 / (lanes * quarter))
    back = inv_scale * (grown - means[:, 0:1] - normed * means[:, 8:9]) + cot_ref[...].astype(F32)
    returning[...] = dot(place[...], back.astype(BF16)).astype(BF16).reshape(groups, cap, quarter)
    each(1, groups, lambda k: back_copy(k).start())
    term_on(1)
    mixed_in[lane] = mixed_part[:, span(lane, quarter)]
    each(1, lanes, lambda k: mixed_copy(k).wait())
    mixed = mixed_in[0].astype(F32)
    for k in range(1, lanes):
        mixed = mixed + mixed_in[k].astype(F32)
    out_ref[...] = (local[...].astype(F32) + mixed).astype(BF16)
    grad_project_ref[...] = term_end(2)

    small_in[me] = small_out[...]
    each(1, groups, lambda k: small_copy(k).wait())
    small = small_in[0]
    for k in range(1, groups):
        small = small + small_in[k]
    small_ref[...] = small * scale

    returned[me] = returning[me]
    each(1, groups, lambda k: back_copy(k).wait())
    back_ref[...] = dot(pick[...], returned[...].reshape(slots, quarter), TN).astype(BF16)

    grad_expand_ref[0] = term_end(0)
    grad_expand_ref[1] = term_end(1)
    for u in range(3):
        each(1, outers, lambda k: term_outer(u, k).wait_send())
        each(0, outers, lambda k: term_pair(u, k).wait_send())


def shards(frames, owner_slot, segment, norm_gain, expand, kernel, project, cotangent):
    rows, quarter = frames.shape
    groups, lanes = lax.axis_size("dp"), lax.axis_size("seq")
    cap = max(16, rows // groups)
    slots = groups * cap
    depth = D // groups
    outers = groups // 2
    inv_root = 1.0 / math.sqrt(rows * groups)
    vmem = pl.BlockSpec(memory_space=pltpu.VMEM)

    def sems(count):
        return pltpu.SemaphoreType.DMA((2, count))

    def terms(count):
        return pltpu.VMEM((3, count, depth, quarter), BF16)

    share = pltpu.VMEM((rows, quarter), F32)
    padded = pltpu.VMEM((rows + 16, quarter), F32)
    all_columns = pltpu.VMEM((rows, D), BF16)
    buckets = pltpu.VMEM((groups, cap, quarter), BF16)
    lane_parts = pltpu.VMEM((lanes, rows, quarter), BF16)
    choice = pltpu.VMEM((slots, rows), BF16)
    output, grad_frames, small, grad_expand, grad_project = pl.pallas_call(
        functools.partial(block_kernel, groups, lanes, cap, inv_root),
        out_shape=(
            jax.ShapeDtypeStruct((rows, quarter), BF16),
            jax.ShapeDtypeStruct((rows, quarter), BF16),
            jax.ShapeDtypeStruct((16, quarter), F32),
            jax.ShapeDtypeStruct((2, depth, quarter), F32),
            jax.ShapeDtypeStruct((depth, quarter), F32),
        ),
        in_specs=[vmem] * 8,
        out_specs=(vmem,) * 5,
        scratch_shapes=[
            pltpu.VMEM((8, rows), jnp.int32), pltpu.VMEM((rows + 16, 128), F32),
            buckets, buckets, pltpu.VMEM((groups, 8, rows), jnp.int32), choice, choice,
            pltpu.VMEM((rows, quarter), BF16), all_columns, all_columns, all_columns,
            terms(groups),
            padded, padded, share, share, share, all_columns, all_columns,
            terms(groups), terms(outers), terms(outers), terms(outers),
            lane_parts, lane_parts,
            pltpu.VMEM((groups, 16, quarter), F32), pltpu.VMEM((16, quarter), F32),
            pltpu.VMEM((lanes, 16, rows), F32), pltpu.VMEM((16, rows), F32),
            buckets, buckets,
            sems(groups), sems(groups), sems(lanes), sems(lanes),
            sems(3 * outers), sems(3 * outers), sems(3 * outers), sems(3 * outers),
            sems(lanes), sems(lanes), sems(groups), sems(lanes), sems(groups),
        ],
        compiler_params=pltpu.CompilerParams(collective_id=0, has_side_effects=True, vmem_limit_bytes=58 << 20),
        name="conv_block",
    )(
        owner_slot[None, :], segment, frames, expand.transpose(1, 0, 2), project.T, cotangent,
        norm_gain[None, :], kernel,
    )
    return (
        output,
        grad_frames,
        small[KSIZE],
        small[:KSIZE],
        grad_expand.transpose(1, 0, 2),
        grad_project.T,
    )


def solution(mesh):
    placed = (
        P("dp", "seq"),
        P("dp"),
        P("dp", None),
        P(),
        P("dp", None, "seq"),
        P(None, "seq"),
        P("seq", "dp"),
        P("dp", "seq"),
    )
    return jax.shard_map(
        shards,
        mesh=mesh,
        in_specs=placed,
        out_specs=(
            P("dp", "seq"),
            P("dp", "seq"),
            P("seq"),
            P(None, "seq"),
            P("dp", None, "seq"),
            P("seq", "dp"),
        ),
        check_vma=False,
    )
```

time: 157 us -> 143 us (0.911); the launches traced: 157 us -> 141 us
  Pallas kernels: 142 us -> 130 us
  local copies, waits for them, and re-layouts: 12.4 us -> 9.9 us
    pallas_call x1, Pallas kernels: 142 us -> 130 us  [shards(): pl.pallas_call(functools.partial(block_kernel, groups, lanes, cap, inv_ro...]
    unnamed x15 -> x14, local copies, waits for them, and re-layouts: 3.97 us -> 7.31 us
    reshape x1 -> x0, local copies, waits for them, and re-layouts: 2.25 us -> none  [shards(): grad_expand.reshape(depth, 2, quarter)]
    broadcast_in_dim x2 -> x0, local copies, waits for them, and re-layouts: 1.85 us -> none  [the longest x1 1.29 us: shards(): owner_rows = jnp.broadcast_to(owner_slot[None, :], (8, rows))]
where the time goes in v3:
time: 143 us; the launch traced here: 141 us
  Pallas kernels  130 us (91%)
  local copies, waits for them, and re-layouts  9.9 us (7%)
    pallas_call x1, Pallas kernels, shards(): pl.pallas_call(functools.partial(block_kernel, groups, lanes, cap, inv_ro...  130 us
    unnamed x14, local copies, waits for them, and re-layouts  7.31 us

profile of v3, /device:TPU:9, one launch (start us, length us, event | category | flops | bytes accessed | tf_op | source)
XLA Modules:
  0.0 140.9 jit_solution(12329243482604649154)
XLA Ops:
  0.6 1.3 broadcast_in_dim.7.gain_ref
  1.9 1.7 %copy.17 = bf16[192,2,384]{2,0,1:T(8,128)(2,1)} copy(bf16[192,2,384]{2,1,0:T(2,128)(2,1)} %param.12) | data formatting | bytes 589824 | tf_op args[4]
  3.6 130.3 %conv_block.1 = (bf16[512,384]{1,0:T(8,128)(2,1)}, bf16[512,384]{1,0:T(8,128)(2,1)}, f32[16,384]{1,0:T(8,128)}, f32[2,192,384]{2,1,0:T(8,128)}, f32[192,384]{1,0:T(8,128)}) custom-call(s32[1,512]{1,0:T(1,128)} %bitcast.13, s32[1,512]{1,0:T(1,128)} %segment_ref.1, bf16[512,384]{1,0:T(8,128)(2,1)} %frames_ref.1, bf16[2,192,384]{2,1,0:T(8,128)(2,1)} %bitcast.8, ...), custom_call_target="tpu_custom_call" | custom-call | tf_op jit(solution)/shard_map/conv_block/pallas_call | solution.py:368
  134.0 1.3 slice_reduce_fusion
  135.3 0.0 copy-start.1
  135.3 2.4 %copy.15 = f32[192,2,384]{2,1,0:T(2,128)} copy(f32[192,2,384]{2,0,1:T(8,128)} %bitcast.9) | data formatting | bytes 1179648
  137.7 0.0 copy-done.1
  137.7 0.0 copy-start
  137.7 0.7 copy.22
  138.4 0.4 copy-done
  138.8 0.0 copy-start.3
  138.8 0.0 copy-start.2
  138.8 0.7 copy.23
  139.6 0.0 copy-done.3
  139.6 0.6 copy.24
  140.2 0.0 copy-done.2
  140.2 0.7 copy.25
Async XLA Ops:
  135.3 2.4 %copy-start.1 = (bf16[512,384]{1,0:T(8,128)(2,1)S(1)}, bf16[512,384]{1,0:T(8,128)(2,1)}, u32[]{:S(2)}) copy-start(bf16[512,384]{1,0:T(8,128)(2,1)} %get-tuple-element.28) | copy-start | bytes 1179652
  137.7 1.1 copy-start
  138.8 0.8 copy-start.3
  138.8 1.4 copy-start.2
